TPU v7x, 256 devices: a whole 4x4x8 slice. The times are simulated.
256 devices in a mesh: row: 16 (over z, core), col: 16 (over y, x).
Axes of the slice: x: 4, y: 4, z: 8, core: 2. Of those that a mesh axis runs over, the one named last changes fastest.
Arguments:
- covariance: float32 [8, 16, 8, 16, 128, 128], P(None, 'row', None, 'col'), as said below
Outputs:
- panel_factor: float32 [8, 16, 6, 128, 128], P(None, 'row')
- trailing: float32 [8, 16, 8, 16, 128, 128], P(None, 'row', None, 'col')
- logdet_mean: float32 [], replicated
Inputs may be any that keep to these rules, and one draw needn't show every extreme that they name: `covariance`: the 16384 x 16384 matrix A assembled from the tiles is symmetric and positive definite, every eigenvalue 0.5 or more.
All inputs are finite; a program needn't handle non-finite values.
Results may differ from a plain program's by a relative error of at most 0.0054.
Values may be sent and summed in bfloat16 or wider, within the bound.
No kernel may reach another device: no remote copies, remote signals or barrier semaphores. Data moves between devices by JAX's collectives and lax.ppermute only.
A program may use at most 128 MiB of HBM per device.

v0:
```python
import jax
import jax.numpy as jnp
from jax import lax
from jax.sharding import PartitionSpec as P

STEPS = 6


def spread(x, axis, root):
    mine = lax.axis_index(axis) == root
    return lax.psum(jnp.where(mine, x, jnp.zeros_like(x)), axis)


def update_columns(block, rounded, columns):
    return block - jnp.einsum("lab,mcb->lmac", rounded, columns, preferred_element_type=jnp.float32)


def shards(covariance):
    row_count = lax.axis_size("row")
    col_count = lax.axis_size("col")
    row_index = lax.axis_index("row")
    col_index = lax.axis_index("col")
    row_tiles = covariance.shape[0]
    col_tiles = covariance.shape[2]
    tile_width = covariance.shape[4]
    row_ratio = row_count // col_count
    matrix = covariance[:, 0, :, 0]
    global_rows = (jnp.arange(row_tiles, dtype=jnp.int32) * row_count + row_index)[:, None, None]
    panels = []
    pivots = []
    for section in range(STEPS):
        owner_row = section % row_count
        owner_col = section % col_count
        local_row = section // row_count
        local_col = section // col_count
        corner = spread(matrix[local_row, local_col], "row", owner_row)
        factor_tile = jnp.linalg.cholesky(corner)
        stacked = matrix[:, local_col].reshape(row_tiles * tile_width, tile_width)
        solved = jax.scipy.linalg.solve_triangular(factor_tile, stacked.T, lower=True).T
        solved = solved.reshape(row_tiles, tile_width, tile_width)
        column_panel = jnp.where(
            global_rows > section, solved, jnp.where(global_rows == section, factor_tile[None], 0.0)
        )
        pivots.append(
            jnp.where(col_index == owner_col, jnp.sum(jnp.log(jnp.diagonal(factor_tile))), 0.0)
        )
        column_panel = spread(column_panel, "col", owner_col)
        panels.append(column_panel)
        rounded = column_panel.astype(jnp.bfloat16)
        gathered = lax.all_gather(rounded[None], "row", axis=0, tiled=True)
        grouped = gathered.reshape(row_ratio, col_count, row_tiles, tile_width, tile_width)
        picked = lax.dynamic_index_in_dim(grouped, col_index, 1, keepdims=False)
        across = picked.transpose(1, 0, 2, 3).reshape(col_tiles, tile_width, tile_width)
        matrix = update_columns(matrix, rounded, across)
    summed = lax.psum(jnp.stack(pivots), "col")
    logdet_mean = 2.0 * jnp.sum(summed) / (STEPS * tile_width)
    panel_factor = jnp.stack(panels, axis=1)[:, None]
    trailing = matrix[:, None, :, None]
    return (panel_factor, trailing, logdet_mean)


def solution(mesh):
    in_specs = (P(None, "row", None, "col", None, None),)
    out_specs = (P(None, "row", None, None, None), P(None, "row", None, "col", None, None), P())
    return jax.shard_map(shards, mesh=mesh, in_specs=in_specs, out_specs=out_specs, check_vma=False)
```

profile of v0, /device:TPU:1, one launch (start us, length us, event | category | flops | bytes accessed | tf_op | source)
XLA Modules:
  0.0 1651.0 jit_solution(13066834229229785264)
XLA Ops:
  15.4 101.9 %all-reduce.13.cloned.1.call-done = f32[128,128]{0,1:T(8,128)} async-done(((f32[128,128]{0,1:T(8,128)}), f32[128,128]{0,1:T(8,128)}) %all-reduce.13.cloned.1.call-update) | async-done | bytes 65552 | tf_op jit(solution)/shard_map/psum | solution.py:11
  119.1 11.7 cholesky.104
  143.8 92.2 %all-reduce.15.cloned.1.call-done = f32[8,128,128]{2,1,0:T(8,128)} async-done(((f32[8,128,128]{2,1,0:T(8,128)}), f32[8,128,128]{2,1,0:T(8,128)}) %all-reduce.15.cloned.1.call-update) | async-done | bytes 524304 | tf_op jit(solution)/shard_map/psum | solution.py:11
  237.9 43.8 %all-gather.13.cloned.1.call-done = bf16[128,128,128]{2,1,0:T(8,128)(2,1)} async-done(((bf16[8,128,128]{2,1,0:T(8,128)(2,1)}), bf16[128,128,128]{2,1,0:T(8,128)(2,1)}) %all-gather.13.cloned.1.call-update) | async-done | bytes 4194320 | tf_op jit(solution)/shard_map/all_gather | solution.py:50
  289.0 96.0 %all-reduce.17.cloned.1.call-done = f32[128,128]{0,1:T(8,128)} async-done(((f32[128,128]{0,1:T(8,128)}), f32[128,128]{0,1:T(8,128)}) %all-reduce.17.cloned.1.call-update) | async-done | bytes 65552 | tf_op jit(solution)/shard_map/psum | solution.py:11
  386.9 11.7 cholesky.115
  411.6 92.2 %all-reduce.19.cloned.1.call-done = f32[8,128,128]{2,1,0:T(8,128)} async-done(((f32[8,128,128]{2,1,0:T(8,128)}), f32[8,128,128]{2,1,0:T(8,128)}) %all-reduce.19.cloned.1.call-update) | async-done | bytes 524304 | tf_op jit(solution)/shard_map/psum | solution.py:11
  505.7 43.7 %all-gather.15.cloned.1.call-done = bf16[128,128,128]{2,1,0:T(8,128)(2,1)} async-done(((bf16[8,128,128]{2,1,0:T(8,128)(2,1)}), bf16[128,128,128]{2,1,0:T(8,128)(2,1)}) %all-gather.15.cloned.1.call-update) | async-done | bytes 4194320 | tf_op jit(solution)/shard_map/all_gather | solution.py:50
  556.7 96.0 %all-reduce.21.cloned.1.call-done = f32[128,128]{0,1:T(8,128)} async-done(((f32[128,128]{0,1:T(8,128)}), f32[128,128]{0,1:T(8,128)}) %all-reduce.21.cloned.1.call-update) | async-done | bytes 65552 | tf_op jit(solution)/shard_map/psum | solution.py:11
  654.5 11.7 cholesky.126
  679.3 92.2 %all-reduce.23.cloned.1.call-done = f32[8,128,128]{2,1,0:T(8,128)} async-done(((f32[8,128,128]{2,1,0:T(8,128)}), f32[8,128,128]{2,1,0:T(8,128)}) %all-reduce.23.cloned.1.call-update) | async-done | bytes 524304 | tf_op jit(solution)/shard_map/psum | solution.py:11
  773.3 43.8 %all-gather.17.cloned.1.call-done = bf16[128,128,128]{2,1,0:T(8,128)(2,1)} async-done(((bf16[8,128,128]{2,1,0:T(8,128)(2,1)}), bf16[128,128,128]{2,1,0:T(8,128)(2,1)}) %all-gather.17.cloned.1.call-update) | async-done | bytes 4194320 | tf_op jit(solution)/shard_map/all_gather | solution.py:50
  824.5 96.0 %all-reduce.25.cloned.1.call-done = f32[128,128]{0,1:T(8,128)} async-done(((f32[128,128]{0,1:T(8,128)}), f32[128,128]{0,1:T(8,128)}) %all-reduce.25.cloned.1.call-update) | async-done | bytes 65552 | tf_op jit(solution)/shard_map/psum | solution.py:11
  922.3 11.7 cholesky.137
  947.1 92.2 %all-reduce.27.cloned.1.call-done = f32[8,128,128]{2,1,0:T(8,128)} async-done(((f32[8,128,128]{2,1,0:T(8,128)}), f32[8,128,128]{2,1,0:T(8,128)}) %all-reduce.27.cloned.1.call-update) | async-done | bytes 524304 | tf_op jit(solution)/shard_map/psum | solution.py:11
  1041.2 43.7 %all-gather.19.cloned.1.call-done = bf16[128,128,128]{2,1,0:T(8,128)(2,1)} async-done(((bf16[8,128,128]{2,1,0:T(8,128)(2,1)}), bf16[128,128,128]{2,1,0:T(8,128)(2,1)}) %all-gather.19.cloned.1.call-update) | async-done | bytes 4194320 | tf_op jit(solution)/shard_map/all_gather | solution.py:50
  1092.4 95.8 %all-reduce.29.cloned.1.call-done = f32[128,128]{0,1:T(8,128)} async-done(((f32[128,128]{0,1:T(8,128)}), f32[128,128]{0,1:T(8,128)}) %all-reduce.29.cloned.1.call-update) | async-done | bytes 65552 | tf_op jit(solution)/shard_map/psum | solution.py:11
  1190.0 11.7 cholesky.148
  1214.7 92.2 %all-reduce.31.cloned.1.call-done = f32[8,128,128]{2,1,0:T(8,128)} async-done(((f32[8,128,128]{2,1,0:T(8,128)}), f32[8,128,128]{2,1,0:T(8,128)}) %all-reduce.31.cloned.1.call-update) | async-done | bytes 524304 | tf_op jit(solution)/shard_map/psum | solution.py:11
  1308.8 43.7 %all-gather.21.cloned.1.call-done = bf16[128,128,128]{2,1,0:T(8,128)(2,1)} async-done(((bf16[8,128,128]{2,1,0:T(8,128)(2,1)}), bf16[128,128,128]{2,1,0:T(8,128)(2,1)}) %all-gather.21.cloned.1.call-update) | async-done | bytes 4194320 | tf_op jit(solution)/shard_map/all_gather | solution.py:50
  1359.8 96.1 %all-reduce.33.cloned.1.call-done = f32[128,128]{0,1:T(8,128)} async-done(((f32[128,128]{0,1:T(8,128)}), f32[128,128]{0,1:T(8,128)}) %all-reduce.33.cloned.1.call-update) | async-done | bytes 65552 | tf_op jit(solution)/shard_map/psum | solution.py:11
  1457.6 11.7 cholesky.159
  1482.4 92.2 %all-reduce.35.cloned.1.call-done = f32[8,128,128]{2,1,0:T(8,128)} async-done(((f32[8,128,128]{2,1,0:T(8,128)}), f32[8,128,128]{2,1,0:T(8,128)}) %all-reduce.35.cloned.1.call-update) | async-done | bytes 524304 | tf_op jit(solution)/shard_map/psum | solution.py:11
  1597.0 31.3 %psum.103 = f32[6]{0:T(128)S(1)} all-reduce(f32[6]{0:T(128)S(1)} %stack.55), channel_id=1, replica_groups=mesh['row'=16,'col'=16] {'col'}, use_global_device_ids=true, to_apply=%region_20.23 | all-reduce | flops 6 | bytes 48 | tf_op jit(solution)/shard_map/psum | solution.py:55
  (163 shorter events, 175.0 us)
Async XLA Ops:
  7.2 110.1 %all-reduce.13.cloned.1.call-start = ((), (), s32[]{:S(2)}) async-start(), calls=%async_computation | async-start | bytes 131072 | tf_op jit(solution)/shard_map/psum | solution.py:11
  14.1 222.0 %all-reduce.15.cloned.1.call-start = ((), (), s32[]{:S(2)}) async-start(), calls=%async_computation.1 | async-start | bytes 1048576 | tf_op jit(solution)/shard_map/psum | solution.py:11
  143.8 138.0 %all-gather.13.cloned.1.call-start = ((), (), s32[]{:S(2)}) async-start(), calls=%async_computation.12 | async-start | bytes 4456448 | tf_op jit(solution)/shard_map/all_gather | solution.py:50
  237.9 147.2 %all-reduce.17.cloned.1.call-start = ((), (), s32[]{:S(2)}) async-start(), calls=%async_computation.2 | async-start | bytes 131072 | tf_op jit(solution)/shard_map/psum | solution.py:11
  284.8 2.0 copy-start.1
  287.5 216.3 %all-reduce.19.cloned.1.call-start = ((), (), s32[]{:S(2)}) async-start(), calls=%async_computation.3 | async-start | bytes 1048576 | tf_op jit(solution)/shard_map/psum | solution.py:11
  411.6 137.8 %all-gather.15.cloned.1.call-start = ((), (), s32[]{:S(2)}) async-start(), calls=%async_computation.13 | async-start | bytes 4456448 | tf_op jit(solution)/shard_map/all_gather | solution.py:50
  505.6 147.1 %all-reduce.21.cloned.1.call-start = ((), (), s32[]{:S(2)}) async-start(), calls=%async_computation.4 | async-start | bytes 131072 | tf_op jit(solution)/shard_map/psum | solution.py:11
  552.4 2.0 copy-start.2
  555.1 216.4 %all-reduce.23.cloned.1.call-start = ((), (), s32[]{:S(2)}) async-start(), calls=%async_computation.5 | async-start | bytes 1048576 | tf_op jit(solution)/shard_map/psum | solution.py:11
  679.2 138.0 %all-gather.17.cloned.1.call-start = ((), (), s32[]{:S(2)}) async-start(), calls=%async_computation.14 | async-start | bytes 4456448 | tf_op jit(solution)/shard_map/all_gather | solution.py:50
  773.3 147.2 %all-reduce.25.cloned.1.call-start = ((), (), s32[]{:S(2)}) async-start(), calls=%async_computation.6 | async-start | bytes 131072 | tf_op jit(solution)/shard_map/psum | solution.py:11
  820.3 2.0 copy-start.3
  822.9 216.4 %all-reduce.27.cloned.1.call-start = ((), (), s32[]{:S(2)}) async-start(), calls=%async_computation.7 | async-start | bytes 1048576 | tf_op jit(solution)/shard_map/psum | solution.py:11
  947.0 137.8 %all-gather.19.cloned.1.call-start = ((), (), s32[]{:S(2)}) async-start(), calls=%async_computation.15 | async-start | bytes 4456448 | tf_op jit(solution)/shard_map/all_gather | solution.py:50
  1041.1 147.1 %all-reduce.29.cloned.1.call-start = ((), (), s32[]{:S(2)}) async-start(), calls=%async_computation.8 | async-start | bytes 131072 | tf_op jit(solution)/shard_map/psum | solution.py:11
  1087.9 2.0 copy-start.4
  1090.6 216.4 %all-reduce.31.cloned.1.call-start = ((), (), s32[]{:S(2)}) async-start(), calls=%async_computation.9 | async-start | bytes 1048576 | tf_op jit(solution)/shard_map/psum | solution.py:11
  1214.7 137.8 %all-gather.21.cloned.1.call-start = ((), (), s32[]{:S(2)}) async-start(), calls=%async_computation.16 | async-start | bytes 4456448 | tf_op jit(solution)/shard_map/all_gather | solution.py:50
  1308.8 147.1 %all-reduce.33.cloned.1.call-start = ((), (), s32[]{:S(2)}) async-start(), calls=%async_computation.10 | async-start | bytes 131072 | tf_op jit(solution)/shard_map/psum | solution.py:11
  1355.6 2.0 copy-start
  1358.2 216.3 %all-reduce.35.cloned.1.call-start = ((), (), s32[]{:S(2)}) async-start(), calls=%async_computation.11 | async-start | bytes 1048576 | tf_op jit(solution)/shard_map/psum | solution.py:11
  1482.3 150.2 %all-gather.23.cloned.1.call-start = ((), (), s32[]{:S(2)}) async-start(), calls=%async_computation.17 | async-start | bytes 4456448 | tf_op jit(solution)/shard_map/all_gather | solution.py:50
  1595.9 36.6 %copy-start.5 = (bf16[8,128,128]{2,1,0:T(8,128)(2,1)S(1)}, bf16[8,128,128]{2,1,0:T(8,128)(2,1)}, u32[]{:S(2)}) copy-start(bf16[8,128,128]{2,1,0:T(8,128)(2,1)} %convert_element_type.23) | copy-start | bytes 786436
Sparse Core Ops, SparseCore 0:
  14.2 103.0 all-reduce.12
  143.9 92.1 all-reduce.14
  238.5 43.2 all-gather.12
  287.6 97.4 all-reduce.16
  411.7 92.1 all-reduce.18
  506.1 43.2 all-gather.14
  555.2 97.4 all-reduce.20
  679.3 92.1 all-reduce.22
  773.9 43.2 all-gather.16
  823.0 97.4 all-reduce.24
  947.1 92.1 all-reduce.26
  1041.6 43.2 all-gather.18
  1090.7 97.4 all-reduce.28
  1214.8 92.1 all-reduce.30
  1309.2 43.2 all-gather.20
  1358.4 97.4 all-reduce.32
  1482.4 92.0 all-reduce.34
  1576.5 43.6 all-gather.22
where the time goes:
time: 1670 us; the launch traced here: 1650 us
  waiting for transfers between devices  1350 us (81%)
  other arithmetic  168 us (10%)
  local copies, waits for them, and re-layouts  51 us (3%)
  blocking collectives  31.3 us (2%)
  matrix products  24.1 us (1%)
  between operations  20.7 us (1%)
    psum x12, waiting for transfers between devices, spread(): return lax.psum(jnp.where(mine, x, jnp.zeros_like(x)), axis)  1140 us
    all_gather x6, waiting for transfers between devices, shards(): gathered = lax.all_gather(rounded[None], 'row', axis=0, tiled=True)  219 us
    another operation x18, other arithmetic, shards(): factor_tile = jnp.linalg.cholesky(corner)  74.3 us
    another operation x12, other arithmetic, shards(): jax.scipy.linalg.solve_triangular(factor_tile, stacked.T, lower=True)  62.8 us
  transfers between devices with their start and end apart: 18, of which 17 were waited for; matrix products, arithmetic and copies ran while one was open for 2% of the time, Pallas kernels for 0%

commit v1 on v0

v1 whole, which is shorter than its diff:
```python
import jax
import jax.numpy as jnp
from jax import lax
from jax.experimental import pallas as pl
from jax.experimental.pallas import tpu as pltpu
from jax.sharding import PartitionSpec as P

STEPS = 6
NB = 128
LT = 8
SB = 16
UPPER = STEPS * (STEPS + 1) // 2


def split2(x):
    hi = x.astype(jnp.bfloat16)
    lo = (x - hi.astype(jnp.float32)).astype(jnp.bfloat16)
    return hi, lo

def chain_kernel(d_ref, ub_ref, linv_ref, logdet_ref, w_ref):
    ub_ref[...] = jnp.zeros_like(ub_ref)
    eye = (lax.broadcasted_iota(jnp.int32, (NB, NB), 0) == lax.broadcasted_iota(jnp.int32, (NB, NB), 1)).astype(jnp.float32)
    rows16 = lax.broadcasted_iota(jnp.int32, (SB, NB), 0)
    def step(k, logs):
        kk = pl.multiple_of(k * NB, NB)
        left = ub_ref[:, pl.ds(kk, NB)]
        for t in range(STEPS):
            j = lax.rem(k + t, STEPS)
            jj = pl.multiple_of(j * NB, NB)
            low, high = jnp.minimum(k, j), jnp.maximum(k, j)
            place = low * STEPS - low * (low - 1) // 2 + high - low
            upd = lax.dot_general(left, ub_ref[:, pl.ds(jj, NB)], (((0,), (0,)), ((), ())), preferred_element_type=jnp.float32)
            w_ref[:, t * NB:(t + 1) * NB] = d_ref[:, place].reshape(NB, NB) - upd
        w_ref[:, STEPS * NB:] = eye
        for s in range(NB // SB):
            r0 = s * SB
            nl = STEPS + 1
            R = [w_ref[r0:r0 + SB, t * NB:(t + 1) * NB] for t in range(nl)]
            cols = [jnp.broadcast_to(R[0][:, r0 + p:r0 + p + 1], (SB, NB)) for p in range(SB)]
            for p in range(SB):
                inv = lax.rsqrt(jnp.broadcast_to(cols[p][p:p + 1, :], (SB, NB)))
                l = cols[p] * inv
                below = rows16 > p
                lm = jnp.where(below, l, 0.0)
                for q in range(p + 1, SB):
                    cols[q] = cols[q] - lm * jnp.broadcast_to(l[q:q + 1, :], (SB, NB))
                for t in range(nl):
                    u = jnp.broadcast_to(R[t][p:p + 1, :], (SB, NB)) * inv
                    R[t] = jnp.where(rows16 == p, u, R[t] - lm * u)
            for t in range(nl):
                w_ref[r0:r0 + SB, t * NB:(t + 1) * NB] = R[t]
            if s < NB // SB - 1:
                X = jnp.concatenate(R, axis=1)
                xhi, xlo = split2(X)
                r1 = r0 + SB
                lh, ll = xhi[:, :NB], xlo[:, :NB]
                L = jnp.concatenate([lh, lh, ll], axis=0)
                Rr = jnp.concatenate([xhi, xlo, xhi], axis=0)
                upd = lax.dot_general(L, Rr, (((0,), (0,)), ((), ())), preferred_element_type=jnp.float32)
                w_ref[r1:, :] = w_ref[r1:, :] - upd[r1:, :]
        tri = lax.broadcasted_iota(jnp.int32, (NB, NB), 0) <= lax.broadcasted_iota(jnp.int32, (NB, NB), 1)
        for t in range(STEPS):
            j = lax.rem(k + t, STEPS)
            jj = pl.multiple_of(j * NB, NB)
            keep = k + t < STEPS
            x = w_ref[:, t * NB:(t + 1) * NB]
            if t == 0:
                x = jnp.where(tri, x, 0.0)
                logs = logs + jnp.sum(jnp.log(jnp.sum(x * eye, axis=0, keepdims=True)), axis=1, keepdims=True)
            else:
                x = jnp.where(keep, x, 0.0)
            ub_ref[pl.ds(kk, NB), pl.ds(jj, NB)] = x.astype(jnp.bfloat16)
        linv_ref[k] = w_ref[:, STEPS * NB:]
        return logs
    logs = lax.fori_loop(0, STEPS, step, jnp.zeros((1, 1), jnp.float32))
    logdet_ref[...] = logs * (2.0 / (STEPS * NB))

def chain(d):
    return pl.pallas_call(
        chain_kernel,
        out_shape=(jax.ShapeDtypeStruct((STEPS * NB, STEPS * NB), jnp.bfloat16),
                   jax.ShapeDtypeStruct((STEPS, NB, NB), jnp.float32),
                   jax.ShapeDtypeStruct((1, 1), jnp.float32)),
        in_specs=[pl.BlockSpec(memory_space=pltpu.VMEM)],
        out_specs=(pl.BlockSpec(memory_space=pltpu.VMEM),) * 3,
        scratch_shapes=[pltpu.VMEM((NB, (STEPS + 1) * NB), jnp.float32)],
        compiler_params=pltpu.CompilerParams(vmem_limit_bytes=48 * 2**20),
        name="chain",
    )(d)


def finish_kernel(place_ref, a_hbm, rp_ref, cp_ref, ub_ref, linv_ref, pf_hbm, tr_hbm, a_ref, p_ref, b_ref, q_ref, in_sem, p_sem, t_sem):
    row = place_ref[0]
    col = place_ref[1]
    loads = [pltpu.make_async_copy(a_hbm.at[l], a_ref.at[l], in_sem.at[l]) for l in range(LT)]
    for c in loads:
        c.start()
    ri = lax.broadcasted_iota(jnp.int32, (NB, NB), 0)
    ci = lax.broadcasted_iota(jnp.int32, (NB, NB), 1)
    stores = []
    for k in range(STEPS):
        lhi, llo = split2(linv_ref[k])
        s = jnp.concatenate([rp_ref[l, k] for l in range(LT)], axis=0)
        if k:
            s = s - jnp.dot(b_ref[:, :k * NB], ub_ref[:k * NB, k * NB:(k + 1) * NB], preferred_element_type=jnp.float32)
        shi, slo = split2(s)
        p = lax.dot_general(jnp.concatenate([shi, shi, slo], axis=1), jnp.concatenate([lhi, llo, lhi], axis=1),
                            (((1,), (1,)), ((), ())), preferred_element_type=jnp.float32)
        keep = jnp.where(row == k, ri - ci, row - k) >= 0
        first = jnp.where(keep, p[:NB], 0.0)
        p_ref[0, k] = first
        for l in range(1, LT):
            p_ref[l, k] = p[l * NB:(l + 1) * NB]
        b_ref[:NB, k * NB:(k + 1) * NB] = first.astype(jnp.bfloat16)
        b_ref[NB:, k * NB:(k + 1) * NB] = p[NB:].astype(jnp.bfloat16)
        st = pltpu.make_async_copy(p_ref.at[:, k], pf_hbm.at[:, k], p_sem.at[k])
        st.start()
        stores.append(st)
        s = jnp.concatenate([cp_ref[k, m].astype(jnp.float32) for m in range(LT)], axis=1)
        if k:
            s = s - lax.dot_general(ub_ref[:k * NB, k * NB:(k + 1) * NB], q_ref[:k * NB, :], (((0,), (0,)), ((), ())),
                                    preferred_element_type=jnp.float32)
        shi, slo = split2(s)
        q = jnp.dot(jnp.concatenate([lhi, lhi, llo], axis=1), jnp.concatenate([shi, slo, shi], axis=0),
                    preferred_element_type=jnp.float32)
        keep = jnp.where(col == k, ci - ri, col - k) >= 0
        q_ref[k * NB:(k + 1) * NB, :NB] = jnp.where(keep, q[:, :NB], 0.0).astype(jnp.bfloat16)
        q_ref[k * NB:(k + 1) * NB, NB:] = q[:, NB:].astype(jnp.bfloat16)
    for l in range(LT):
        loads[l].wait()
        upd = jnp.dot(b_ref[l * NB:(l + 1) * NB, :], q_ref[...], preferred_element_type=jnp.float32)
        for m in range(LT):
            a_ref[l, m] = a_ref[l, m] - upd[:, m * NB:(m + 1) * NB]
        st = pltpu.make_async_copy(a_ref.at[l], tr_hbm.at[l], t_sem.at[l])
        st.start()
        stores.append(st)
    for st in stores:
        st.wait()

def finish(place, a, rp, cp, ub, linv):
    vm = pl.BlockSpec(memory_space=pltpu.VMEM)
    hb = pl.BlockSpec(memory_space=pl.ANY)
    return pl.pallas_call(
        finish_kernel,
        out_shape=(jax.ShapeDtypeStruct((LT, STEPS, NB, NB), jnp.float32),
                   jax.ShapeDtypeStruct((LT, LT, NB, NB), jnp.float32)),
        in_specs=[pl.BlockSpec(memory_space=pltpu.SMEM), hb, vm, vm, vm, vm],
        out_specs=(hb, hb),
        scratch_shapes=[pltpu.VMEM((LT, LT, NB, NB), jnp.float32), pltpu.VMEM((LT, STEPS, NB, NB), jnp.float32),
                        pltpu.VMEM((LT * NB, STEPS * NB), jnp.bfloat16), pltpu.VMEM((STEPS * NB, LT * NB), jnp.bfloat16),
                        pltpu.SemaphoreType.DMA((LT,)), pltpu.SemaphoreType.DMA((STEPS,)), pltpu.SemaphoreType.DMA((LT,))],
        compiler_params=pltpu.CompilerParams(vmem_limit_bytes=48 * 2**20),
        name="finish",
    )(place, a, rp, cp, ub, linv)


def diagonal_block(tile):
    slabs = lax.all_to_all(tile, "row", 0, 0, tiled=True).reshape(16, 8, NB)[:STEPS]
    spread = jnp.broadcast_to(slabs[None], (16, STEPS, 8, NB)).reshape(16 * STEPS * 8, NB)
    slabs = lax.all_to_all(spread, "col", 0, 0, tiled=True).reshape(16, STEPS, 8, NB)
    upper = jnp.stack([slabs[q, p] for p in range(STEPS) for q in range(p, STEPS)])
    spread = jnp.broadcast_to(upper[None], (16,) + upper.shape).reshape(-1, NB)
    return lax.all_to_all(spread, "row", 0, 0, tiled=True).reshape(16, UPPER, 8, NB)


def shards(covariance):
    matrix = covariance[:, 0, :, 0]
    corner = diagonal_block(matrix[0, 0])
    across = lax.all_gather(matrix[0], "row", axis=0, tiled=False)[:STEPS]
    down = lax.all_gather(matrix[:, 0], "col", axis=1, tiled=False)[:, :STEPS]
    ub, linv, logdet = chain(corner)
    place = jnp.stack([lax.axis_index("row"), lax.axis_index("col")]).astype(jnp.int32)
    panel, trailing = finish(place, matrix, down, across, ub, linv)
    return panel[:, None], trailing[:, None, :, None], logdet[0, 0]


def solution(mesh):
    in_specs = (P(None, "row", None, "col", None, None),)
    out_specs = (P(None, "row", None, None, None), P(None, "row", None, "col", None, None), P())
    return jax.shard_map(shards, mesh=mesh, in_specs=in_specs, out_specs=out_specs, check_vma=False)
```

time: 1670 us -> 197 us (0.12); the launches traced: 1650 us -> 196 us
  waiting for transfers between devices: 1350 us -> 95.7 us
  other arithmetic: 168 us -> 0.07 us
  local copies, waits for them, and re-layouts: 51 us -> 12 us
  Pallas kernels: 0 us -> 35.7 us
  matrix products: 24.1 us -> 0 us
    psum x12 -> x0, waiting for transfers between devices: 1140 us -> none  [spread(): return lax.psum(jnp.where(mine, x, jnp.zeros_like(x)), axis)]
    all_gather x6 -> x2, waiting for transfers between devices: 219 us -> 49.6 us  [the longest x1 49.6 us: shards(): down = lax.all_gather(matrix[:, 0], 'col', axis=1, tiled=False)[:, :STEPS]]
    another operation x30 -> x1, other arithmetic: 137 us -> 0.07 us  [shards(): jnp.stack([lax.axis_index('row'), lax.axis_index('col')]).astype(jnp.int32)]
    all_to_all x0 -> x1, waiting for transfers between devices: none -> 46 us  [diagonal_block(): lax.all_to_all(spread, 'row', 0, 0, tiled=True).reshape(16, UPPER, 8, NB)]
    pallas_call x0 -> x2, Pallas kernels: none -> 35.7 us  [the longest x1 24.8 us: chain(): pl.pallas_call(chain_kernel, out_shape=(jax.ShapeDtypeStruct((STEPS * NB,...]
    all_to_all x0 -> x2, blocking collectives: none -> 33.6 us  [the longest x1 17.7 us: diagonal_block(): lax.all_to_all(tile, 'row', 0, 0, tiled=True).reshape(16, 8, NB)[:STEPS]]
    psum x1 -> x0, blocking collectives: 31.3 us -> none  [shards(): summed = lax.psum(jnp.stack(pivots), 'col')]
    unnamed x20, local copies, waits for them, and re-layouts: 28 us -> 0.06 us
  transfers between devices with their start and end apart: 18 -> 3, of which waited for: 17 -> 2; matrix products, arithmetic and copies ran while one was open for 2% -> 4% of each run, Pallas kernels for 0% -> 13%
where the time goes in v1:
time: 197 us; the launch traced here: 196 us
  waiting for transfers between devices  95.7 us (49%)
  Pallas kernels  35.7 us (18%)
  blocking collectives  33.6 us (17%)
  between operations  14.2 us (7%)
  local copies, waits for them, and re-layouts  12 us (6%)
  starting transfers between devices  5.14 us (3%)
    all_gather x1, waiting for transfers between devices, shards(): down = lax.all_gather(matrix[:, 0], 'col', axis=1, tiled=False)[:, :STEPS]  49.6 us
    all_to_all x1, waiting for transfers between devices, diagonal_block(): lax.all_to_all(spread, 'row', 0, 0, tiled=True).reshape(16, UPPER, 8, NB)  46 us
    pallas_call x1, Pallas kernels, chain(): pl.pallas_call(chain_kernel, out_shape=(jax.ShapeDtypeStruct((STEPS * NB,...  24.8 us
    all_to_all x1, blocking collectives, diagonal_block(): lax.all_to_all(tile, 'row', 0, 0, tiled=True).reshape(16, 8, NB)[:STEPS]  17.7 us
    all_to_all x1, blocking collectives, diagonal_block(): lax.all_to_all(spread, 'col', 0, 0, tiled=True).reshape(16, STEPS, 8, NB)  15.9 us
    pallas_call x1, Pallas kernels, finish(): pl.pallas_call(finish_kernel, out_shape=(jax.ShapeDtypeStruct((LT, STEPS,...  11 us
    slice x2, local copies, waits for them, and re-layouts, shards(): across = lax.all_gather(matrix[0], 'row', axis=0, tiled=False)[:STEPS]  5.79 us
    all_to_all x1, starting transfers between devices, diagonal_block(): lax.all_to_all(spread, 'row', 0, 0, tiled=True).reshape(16, UPPER, 8, NB)  5.06 us
  transfers between devices with their start and end apart: 3, of which 2 were waited for; matrix products, arithmetic and copies ran while one was open for 4% of the time, Pallas kernels for 13%

profile of v1, /device:TPU:1, one launch (start us, length us, event | category | flops | bytes accessed | tf_op | source)
XLA Modules:
  0.0 196.5 jit_solution(8683279417063316188)
XLA Ops:
  7.2 0.0 all-gather.6.cloned.1.call-start
  7.2 1.9 slice.88
  9.1 0.0 all-gather.6.cloned.1.call-update
  9.1 0.0 all-gather.4.cloned.1.call-start
  9.2 1.9 slice.115
  11.1 0.0 all-gather.4.cloned.1.call-update
  11.1 0.8 slice_bitcast_fusion.1
  11.9 17.7 %all_to_all.21 = f32[16,8,128]{2,1,0:T(8,128)S(1)} all-to-all(f32[16,8,128]{2,1,0:T(8,128)S(1)} %slice_bitcast_fusion.1), channel_id=1, replica_groups=mesh['row'=16,'col'=16] {'row'}, dimensions={0} | all-to-all | bytes 131072 | tf_op jit(solution)/shard_map/all_to_all | solution.py:158
  29.6 15.9 %all_to_all.22 = f32[16,48,128]{2,1,0:T(8,128)S(1)} all-to-all(f32[16,48,128]{2,1,0:T(8,128)S(1)} %broadcast_in_dim.23), channel_id=1, replica_groups=mesh['row'=16,'col'=16] {'col'}, dimensions={0} | all-to-all | bytes 786432 | tf_op jit(solution)/shard_map/all_to_all | solution.py:160
  45.8 1.2 broadcast_in_dim.25
  46.9 5.1 %all-to-all-start.2 = ((f32[16,168,128]{2,1,0:T(8,128)}), f32[16,168,128]{2,1,0:T(8,128)S(1)}, u32[]{:S(2)}, u32[]{:S(2)}) async-start(f32[16,168,128]{2,1,0:T(8,128)} %broadcast_in_dim.25), calls=%async_computation.2 | async-start | bytes 2752512 | tf_op jit(solution)/shard_map/all_to_all | solution.py:163
  52.0 0.1 pad_add_fusion.place_ref
  52.1 46.0 %all-to-all-done.2 = f32[16,168,128]{2,1,0:T(8,128)S(1)} async-done(((f32[16,168,128]{2,1,0:T(8,128)}), f32[16,168,128]{2,1,0:T(8,128)S(1)}, u32[]{:S(2)}, u32[]{:S(2)}) %all-to-all-start.2) | async-done | bytes 1376288 | tf_op jit(solution)/shard_map/all_to_all | solution.py:163
  98.1 24.8 %chain.1 = (bf16[768,768]{1,0:T(8,128)(2,1)S(1)}, f32[6,128,128]{2,1,0:T(8,128)S(1)}, f32[1,1]{1,0:T(1,128)}) custom-call(f32[16,21,8,128]{3,2,1,0:T(8,128)S(1)} %bitcast.104), custom_call_target="tpu_custom_call" | custom-call | tf_op jit(solution)/shard_map/chain/pallas_call | solution.py:79
  122.9 0.0 all-gather.6.cloned.1.call-done
  122.9 3.9 %slice_bitcast_fusion.cp_ref = f32[6,8,128,128]{3,2,1,0:T(8,128)} fusion(f32[16,1,8,1,128,128]{5,4,2,0,3,1:T(8,128)} %bitcast.108), kind=kLoop, calls=%fused_computation | loop fusion | bytes 6291456 | tf_op jit(solution)/shard_map/slice | solution.py:169
  126.8 49.6 %all-gather.4.cloned.1.call-done = f32[8,16,128,128]{3,2,1,0:T(8,128)} async-done(((f32[8,1,128,128]{3,2,1,0:T(8,128)}), f32[8,16,128,128]{3,2,1,0:T(8,128)}) %all-gather.4.cloned.1.call-update) | async-done | bytes 8388624 | tf_op jit(solution)/shard_map/all_gather | solution.py:170
  176.4 2.2 %slice.116.rp_ref = f32[8,6,128,128]{3,2,1,0:T(8,128)S(1)} slice(f32[8,16,128,128]{3,2,1,0:T(8,128)} %all-gather.4.cloned.1.call-done), slice={[0:8], [0:6], [0:128], [0:128]} | slice | bytes 6291456 | tf_op jit(solution)/shard_map/slice | solution.py:170
  178.7 11.0 %finish.1 = (f32[8,6,128,128]{3,2,1,0:T(8,128)}, f32[8,8,128,128]{3,2,1,0:T(8,128)}) custom-call(s32[2]{0:T(128)S(1)} %pad_add_fusion.place_ref, f32[8,8,128,128]{3,2,1,0:T(8,128)} %bitcast.107, f32[8,6,128,128]{3,2,1,0:T(8,128)S(1)} %slice.116.rp_ref, f32[6,8,128,128]{3,2,1,0:T(8,128)} %slice_bitcast_fusion.cp_ref, ...), custom_call_target="tpu_custom_call" | custom-call | tf_op jit(solution)/shard_map/finish/pallas_call | solution.py:143
  (23 shorter events, 0.1 us)
Async XLA Ops:
  7.2 115.7 %all-gather.6.cloned.1.call-start = ((), (), s32[]{:S(2)}) async-start(), calls=%async_computation.4 | async-start | bytes 8912896 | tf_op jit(solution)/shard_map/all_gather | solution.py:169
  9.1 167.3 %all-gather.4.cloned.1.call-start = ((), (), s32[]{:S(2)}) async-start(), calls=%async_computation.3 | async-start | bytes 8912896 | tf_op jit(solution)/shard_map/all_gather | solution.py:170
  46.9 51.2 %all-to-all-start.2 = ((f32[16,168,128]{2,1,0:T(8,128)}), f32[16,168,128]{2,1,0:T(8,128)S(1)}, u32[]{:S(2)}, u32[]{:S(2)}) async-start(f32[16,168,128]{2,1,0:T(8,128)} %broadcast_in_dim.25), calls=%async_computation.2 | async-start | bytes 2752512 | tf_op jit(solution)/shard_map/all_to_all | solution.py:163
Sparse Core Ops, SparseCore 0:
  9.8 89.6 all-gather.5
  102.5 73.8 all-gather.3

commit v2 on v1

--- a/solution.py
+++ b/solution.py
@@ -9,7 +9,8 @@
 NB = 128
 LT = 8
 SB = 16
-UPPER = STEPS * (STEPS + 1) // 2
+HALF = 12
+SHIFT = 13.0
 
 
 def split2(x):
@@ -17,7 +18,11 @@
     lo = (x - hi.astype(jnp.float32)).astype(jnp.bfloat16)
     return hi, lo
 
-def chain_kernel(d_ref, ub_ref, linv_ref, logdet_ref, w_ref):
+def chain_kernel(place_ref, mine_ref, other_ref, ub_ref, linv_ref, logdet_ref, w_ref, d_ref):
+    core = lax.rem(place_ref[0], 2)
+    for n in range(HALF):
+        d_ref[core, n] = mine_ref[:, n].reshape(NB, NB)
+        d_ref[1 - core, n] = other_ref[:, n].reshape(NB, NB)
     ub_ref[...] = jnp.zeros_like(ub_ref)
     eye = (lax.broadcasted_iota(jnp.int32, (NB, NB), 0) == lax.broadcasted_iota(jnp.int32, (NB, NB), 1)).astype(jnp.float32)
     rows16 = lax.broadcasted_iota(jnp.int32, (SB, NB), 0)
@@ -28,9 +33,10 @@
             j = lax.rem(k + t, STEPS)
             jj = pl.multiple_of(j * NB, NB)
             low, high = jnp.minimum(k, j), jnp.maximum(k, j)
-            place = low * STEPS - low * (low - 1) // 2 + high - low
+            pair = low // 2
+            place = pair * STEPS - pair * (pair - 1) + high - 2 * pair
             upd = lax.dot_general(left, ub_ref[:, pl.ds(jj, NB)], (((0,), (0,)), ((), ())), preferred_element_type=jnp.float32)
-            w_ref[:, t * NB:(t + 1) * NB] = d_ref[:, place].reshape(NB, NB) - upd
+            w_ref[:, t * NB:(t + 1) * NB] = d_ref[lax.rem(low, 2), place] - upd
         w_ref[:, STEPS * NB:] = eye
         for s in range(NB // SB):
             r0 = s * SB
@@ -75,32 +81,34 @@
     logs = lax.fori_loop(0, STEPS, step, jnp.zeros((1, 1), jnp.float32))
     logdet_ref[...] = logs * (2.0 / (STEPS * NB))
 
-def chain(d):
+def chain(place, mine, other):
     return pl.pallas_call(
         chain_kernel,
         out_shape=(jax.ShapeDtypeStruct((STEPS * NB, STEPS * NB), jnp.bfloat16),
                    jax.ShapeDtypeStruct((STEPS, NB, NB), jnp.float32),
                    jax.ShapeDtypeStruct((1, 1), jnp.float32)),
-        in_specs=[pl.BlockSpec(memory_space=pltpu.VMEM)],
+        in_specs=[pl.BlockSpec(memory_space=pltpu.SMEM)] + [pl.BlockSpec(memory_space=pltpu.VMEM)] * 2,
         out_specs=(pl.BlockSpec(memory_space=pltpu.VMEM),) * 3,
-        scratch_shapes=[pltpu.VMEM((NB, (STEPS + 1) * NB), jnp.float32)],
+        scratch_shapes=[pltpu.VMEM((NB, (STEPS + 1) * NB), jnp.float32), pltpu.VMEM((2, HALF, NB, NB), jnp.float32)],
         compiler_params=pltpu.CompilerParams(vmem_limit_bytes=48 * 2**20),
+        cost_estimate=pl.CostEstimate(flops=30_000_000_000, bytes_accessed=4 * 2**20, transcendentals=0),
         name="chain",
-    )(d)
-
-
-def finish_kernel(place_ref, a_hbm, rp_ref, cp_ref, ub_ref, linv_ref, pf_hbm, tr_hbm, a_ref, p_ref, b_ref, q_ref, in_sem, p_sem, t_sem):
+    )(place, mine, other)
+
+
+def finish_kernel(place_ref, a_hbm, rp_ref, cp_hbm, ub_ref, linv_ref, pf_hbm, tr_hbm, a_ref, cp_ref, p_ref, b_ref, q_ref, in_sem, c_sem, p_sem, t_sem):
     row = place_ref[0]
     col = place_ref[1]
     loads = [pltpu.make_async_copy(a_hbm.at[l], a_ref.at[l], in_sem.at[l]) for l in range(LT)]
-    for c in loads:
+    tops = [pltpu.make_async_copy(cp_hbm.at[k], cp_ref.at[k], c_sem.at[k]) for k in range(STEPS)]
+    for c in tops + loads:
         c.start()
     ri = lax.broadcasted_iota(jnp.int32, (NB, NB), 0)
     ci = lax.broadcasted_iota(jnp.int32, (NB, NB), 1)
     stores = []
     for k in range(STEPS):
         lhi, llo = split2(linv_ref[k])
-        s = jnp.concatenate([rp_ref[l, k] for l in range(LT)], axis=0)
+        s = jnp.concatenate([rp_ref[:, k, l].reshape(NB, NB) for l in range(LT)], axis=0)
         if k:
             s = s - jnp.dot(b_ref[:, :k * NB], ub_ref[:k * NB, k * NB:(k + 1) * NB], preferred_element_type=jnp.float32)
         shi, slo = split2(s)
@@ -116,7 +124,8 @@
         st = pltpu.make_async_copy(p_ref.at[:, k], pf_hbm.at[:, k], p_sem.at[k])
         st.start()
         stores.append(st)
-        s = jnp.concatenate([cp_ref[k, m].astype(jnp.float32) for m in range(LT)], axis=1)
+        tops[k].wait()
+        s = jnp.concatenate([cp_ref[k, m] for m in range(LT)], axis=1)
         if k:
             s = s - lax.dot_general(ub_ref[:k * NB, k * NB:(k + 1) * NB], q_ref[:k * NB, :], (((0,), (0,)), ((), ())),
                                     preferred_element_type=jnp.float32)
@@ -144,32 +153,64 @@
         finish_kernel,
         out_shape=(jax.ShapeDtypeStruct((LT, STEPS, NB, NB), jnp.float32),
                    jax.ShapeDtypeStruct((LT, LT, NB, NB), jnp.float32)),
-        in_specs=[pl.BlockSpec(memory_space=pltpu.SMEM), hb, vm, vm, vm, vm],
+        in_specs=[pl.BlockSpec(memory_space=pltpu.SMEM), hb, vm, hb, vm, vm],
         out_specs=(hb, hb),
-        scratch_shapes=[pltpu.VMEM((LT, LT, NB, NB), jnp.float32), pltpu.VMEM((LT, STEPS, NB, NB), jnp.float32),
+        scratch_shapes=[pltpu.VMEM((LT, LT, NB, NB), jnp.float32), pltpu.VMEM((STEPS, LT, NB, NB), jnp.float32),
+                        pltpu.VMEM((LT, STEPS, NB, NB), jnp.float32),
                         pltpu.VMEM((LT * NB, STEPS * NB), jnp.bfloat16), pltpu.VMEM((STEPS * NB, LT * NB), jnp.bfloat16),
-                        pltpu.SemaphoreType.DMA((LT,)), pltpu.SemaphoreType.DMA((STEPS,)), pltpu.SemaphoreType.DMA((LT,))],
+                        pltpu.SemaphoreType.DMA((LT,)), pltpu.SemaphoreType.DMA((STEPS,)),
+                        pltpu.SemaphoreType.DMA((STEPS,)), pltpu.SemaphoreType.DMA((LT,))],
         compiler_params=pltpu.CompilerParams(vmem_limit_bytes=48 * 2**20),
         name="finish",
     )(place, a, rp, cp, ub, linv)
 
 
-def diagonal_block(tile):
-    slabs = lax.all_to_all(tile, "row", 0, 0, tiled=True).reshape(16, 8, NB)[:STEPS]
-    spread = jnp.broadcast_to(slabs[None], (16, STEPS, 8, NB)).reshape(16 * STEPS * 8, NB)
-    slabs = lax.all_to_all(spread, "col", 0, 0, tiled=True).reshape(16, STEPS, 8, NB)
-    upper = jnp.stack([slabs[q, p] for p in range(STEPS) for q in range(p, STEPS)])
-    spread = jnp.broadcast_to(upper[None], (16,) + upper.shape).reshape(-1, NB)
-    return lax.all_to_all(spread, "row", 0, 0, tiled=True).reshape(16, UPPER, 8, NB)
+def spread_kernel(x_ref, o_ref):
+    tiles = [x_ref[p, q] for p in range(STEPS // 2) for q in range(2 * p, STEPS)]
+    for j in range(16):
+        for n, tile in enumerate(tiles):
+            o_ref[j, n] = tile
+
+
+def spread_half(x):
+    return pl.pallas_call(
+        spread_kernel,
+        out_shape=jax.ShapeDtypeStruct((16, HALF, 8, NB), jnp.float32),
+        in_specs=[pl.BlockSpec(memory_space=pltpu.VMEM)],
+        out_specs=pl.BlockSpec(memory_space=pltpu.VMEM),
+        name="spread",
+    )(x)
+
+
+def packed(x):
+    top = jnp.maximum(jnp.max(jnp.abs(x)), 1e-30)
+    power = jnp.floor(jnp.log2(top))
+    body = (x * jnp.exp2(SHIFT - power)).astype(jnp.float16)
+    return jnp.concatenate([body, jnp.full((16, NB), power, jnp.float16)], axis=0)
+
+
+def unpacked(x):
+    power = x[:, -16:-15, :1].astype(jnp.float32)
+    return x[:, :-16].astype(jnp.float32) * jnp.exp2(power - SHIFT)
 
 
 def shards(covariance):
     matrix = covariance[:, 0, :, 0]
-    corner = diagonal_block(matrix[0, 0])
-    across = lax.all_gather(matrix[0], "row", axis=0, tiled=False)[:STEPS]
-    down = lax.all_gather(matrix[:, 0], "col", axis=1, tiled=False)[:, :STEPS]
-    ub, linv, logdet = chain(corner)
-    place = jnp.stack([lax.axis_index("row"), lax.axis_index("col")]).astype(jnp.int32)
+    row = lax.axis_index("row")
+    place = jnp.stack([row, lax.axis_index("col")]).astype(jnp.int32)
+    across = lax.all_gather(matrix[0], "row", axis=0, tiled=False)
+    first = matrix[:, 0].reshape(LT, 16, 8, NB).transpose(1, 0, 2, 3).reshape(16 * LT * 8, NB)
+    slabs = lax.all_to_all(first, "col", 0, 0, tiled=True).reshape(16, LT, 8, NB)[:STEPS]
+    sent = jnp.broadcast_to(slabs[None, :, 0], (8, STEPS, 8, NB))
+    groups = [[2 * z + c for z in range(8)] for c in range(2)]
+    lead = lax.all_to_all(sent, "row", 0, 0, tiled=True, axis_index_groups=groups)
+    mine = lax.all_to_all(spread_half(lead), "col", 0, 0, tiled=True)
+    other = lax.ppermute(mine, "row", [(i, i ^ 1) for i in range(16)])
+    half = packed(slabs.reshape(STEPS * LT * 8, NB))
+    half, other = lax.optimization_barrier((half, other))
+    down = lax.all_to_all(jnp.broadcast_to(half[None], (16,) + half.shape), "col", 0, 0, tiled=True)
+    ub, linv, logdet = chain(place, mine, other)
+    down = unpacked(down).reshape(16, STEPS, LT, 8, NB)
     panel, trailing = finish(place, matrix, down, across, ub, linv)
     return panel[:, None], trailing[:, None, :, None], logdet[0, 0]
 

time: 197 us -> 128 us (0.65)
  waiting for transfers between devices: 95.7 us -> 1.85 us
  blocking collectives: 33.6 us -> 52.9 us
  local copies, waits for them, and re-layouts: 12 us -> 7.55 us
  Pallas kernels: 35.7 us -> 39.2 us
  starting transfers between devices: 5.14 us -> 8.2 us
  other arithmetic: 0.07 us -> 2.54 us
    all_gather x2 -> x1, waiting for transfers between devices: 49.6 us -> 0.02 us  [shards(): across = lax.all_gather(matrix[0], 'row', axis=0, tiled=False)]
    all_to_all x1, waiting for transfers between devices: 46 us -> 0.01 us  [shards(): lax.all_to_all(jnp.broadcast_to(half[None], (16,) + half.shape), 'col', 0...]
    all_to_all x2 -> x3, blocking collectives: 33.6 us -> 52.9 us  [the longest x1 19.9 us: shards(): lax.all_to_all(sent, 'row', 0, 0, tiled=True, axis_index_groups=groups)]
    slice x4 -> x2, local copies, waits for them, and re-layouts: 9.9 us -> 2.66 us  [the longest x1 1.89 us: shards(): across = lax.all_gather(matrix[0], 'row', axis=0, tiled=False)]
    ppermute x0 -> x1, starting transfers between devices: none -> 3.76 us  [shards(): other = lax.ppermute(mine, 'row', [(i, i ^ 1) for i in range(16)])]
    unnamed x20 -> x5, local copies, waits for them, and re-layouts: 0.06 us -> 2.38 us
  transfers between devices with their start and end apart: 3 -> 3, of which waited for: 2 -> 1; matrix products, arithmetic and copies ran while one was open for 4% -> 5% of each run, Pallas kernels for 13% -> 21%
where the time goes in v2:
time: 128 us; the launch traced here: 127 us
  blocking collectives  52.9 us (41%)
  Pallas kernels  39.2 us (31%)
  between operations  14.9 us (12%)
  starting transfers between devices  8.2 us (6%)
  local copies, waits for them, and re-layouts  7.55 us (6%)
  other arithmetic  2.54 us (2%)
  waiting for transfers between devices  1.85 us (1%)
    pallas_call x1, Pallas kernels, chain(): pl.pallas_call(chain_kernel, out_shape=(jax.ShapeDtypeStruct((STEPS * NB,...  25.4 us
    all_to_all x1, blocking collectives, shards(): lax.all_to_all(sent, 'row', 0, 0, tiled=True, axis_index_groups=groups)  19.9 us
    all_to_all x1, blocking collectives, shards(): lax.all_to_all(first, 'col', 0, 0, tiled=True).reshape(16, LT, 8, NB)  17.9 us
    all_to_all x1, blocking collectives, shards(): mine = lax.all_to_all(spread_half(lead), 'col', 0, 0, tiled=True)  15.1 us
    pallas_call x1, Pallas kernels, finish(): pl.pallas_call(finish_kernel, out_shape=(jax.ShapeDtypeStruct((LT, STEPS,...  11.9 us
    all_to_all x1, starting transfers between devices, shards(): lax.all_to_all(jnp.broadcast_to(half[None], (16,) + half.shape), 'col', 0...  4.4 us
    ppermute x1, starting transfers between devices, shards(): other = lax.ppermute(mine, 'row', [(i, i ^ 1) for i in range(16)])  3.76 us
  transfers between devices with their start and end apart: 3, of which 1 were waited for; matrix products, arithmetic and copies ran while one was open for 5% of the time, Pallas kernels for 21%

profile of v2, /device:TPU:1, one launch (start us, length us, event | category | flops | bytes accessed | tf_op | source)
XLA Modules:
  0.0 127.2 jit_solution(16311312590161797616)
XLA Ops:
  7.2 0.0 all-gather.3.cloned.1.call-start
  7.2 1.9 %slice.31 = f32[1,1,8,1,128,128]{5,4,3,2,1,0:T(8,128)} slice(f32[8,1,8,1,128,128]{5,4,3,2,1,0:T(8,128)} %param.1), slice={[0:1], [0:1], [0:8], [0:1], [0:128], [0:128]} | slice | bytes 1048576 | tf_op jit(solution)/shard_map/slice | solution.py:201
  9.1 0.0 all-gather.3.cloned.1.call-update
  9.1 1.1 copy_bitcast_fusion
  10.2 17.9 %all_to_all.24 = f32[16,64,128]{2,1,0:T(8,128)S(1)} all-to-all(f32[16,64,128]{2,1,0:T(8,128)S(1)} %copy_bitcast_fusion), channel_id=1, replica_groups=mesh['row'=16,'col'=16] {'col'}, dimensions={0} | all-to-all | bytes 1048576 | tf_op jit(solution)/shard_map/all_to_all | solution.py:203
  28.1 0.6 abs_reduce_fusion
  29.5 19.9 %all_to_all.25.x_ref = f32[8,6,8,128]{3,2,1,0:T(8,128)} all-to-all(f32[8,6,8,128]{3,2,1,0:T(8,128)S(1)} %broadcast_in_dim.21), channel_id=1, replica_groups={{0,32,64,96,128,160,192,224},{16,48,80,112,144,176,208,240},{1,33,65,97..., dimensions={0} | all-to-all | bytes 393216 | tf_op jit(solution)/shard_map/all_to_all | solution.py:206
  49.5 1.9 %spread.1 = f32[16,12,8,128]{3,2,1,0:T(8,128)} custom-call(f32[8,6,8,128]{3,2,1,0:T(8,128)} %all_to_all.25.x_ref), custom_call_target="tpu_custom_call" | custom-call | tf_op jit(solution)/shard_map/spread/pallas_call | solution.py:176
  51.4 15.1 %all_to_all.26.mine_ref = f32[16,12,8,128]{3,2,1,0:T(8,128)S(1)} all-to-all(f32[16,12,8,128]{3,2,1,0:T(8,128)} %spread.1), channel_id=1, replica_groups=mesh['row'=16,'col'=16] {'col'}, dimensions={0} | all-to-all | bytes 1572864 | tf_op jit(solution)/shard_map/all_to_all | solution.py:207
  66.5 3.8 %collective-permute-start = (f32[16,12,8,128]{3,2,1,0:T(8,128)S(1)}, f32[16,12,8,128]{3,2,1,0:T(8,128)S(1)}, u32[]{:S(2)}, u32[]{:S(2)}) collective-permute-start(f32[16,12,8,128]{3,2,1,0:T(8,128)S(1)} %all_to_all.26.mine_ref), channel_id=1, source_target_pairs={{0,16},{16,0},{32,48},{48,32},{64,80},{80,64},{96,112},{112,96},{1... | collective-permute-start | bytes 2359304 | tf_op jit(solution)/shard_map/ppermute | solution.py:208
  70.3 0.1 pad_add_fusion.place_ref
  70.4 1.8 %collective-permute-done.other_ref = f32[16,12,8,128]{3,2,1,0:T(8,128)S(1)} collective-permute-done((f32[16,12,8,128]{3,2,1,0:T(8,128)S(1)}, f32[16,12,8,128]{3,2,1,0:T(8,128)S(1)}, u32[]{:S(2)}, u32[]{:S(2)}) %collective-permute-start) | collective-permute-done | bytes 786464 | tf_op jit(solution)/shard_map/ppermute | solution.py:208
  72.2 1.4 %broadcast_in_dim.22 = f16[16,400,128]{2,1,0:T(8,128)(2,1)} broadcast(f16[400,128]{1,0:T(8,128)(2,1)S(1)} %concatenate.3), dimensions={1,2} | broadcast | bytes 1740800 | tf_op jit(solution)/shard_map/broadcast_in_dim | solution.py:211
  73.5 4.4 %all-to-all-start.3 = ((f16[16,400,128]{2,1,0:T(8,128)(2,1)}), f16[16,400,128]{2,1,0:T(8,128)(2,1)}, u32[]{:S(2)}, u32[]{:S(2)}) async-start(f16[16,400,128]{2,1,0:T(8,128)(2,1)} %broadcast_in_dim.22), calls=%async_computation.3 | async-start | bytes 3276800 | tf_op jit(solution)/shard_map/all_to_all | solution.py:211
  78.0 25.4 %chain.1 = (bf16[768,768]{1,0:T(8,128)(2,1)S(1)}, f32[6,128,128]{2,1,0:T(8,128)S(1)}, f32[1,1]{1,0:T(1,128)}) custom-call(s32[2]{0:T(128)S(1)} %pad_add_fusion.place_ref, f32[16,12,8,128]{3,2,1,0:T(8,128)S(1)} %all_to_all.26.mine_ref, f32[16,12,8,128]{3,2,1,0:T(8,128)S(1)} %collective-permute-done.other_ref), custom_call_target="tpu_custom_call" | custom-call | flops 30000001024 | bytes 4194304 | tf_op jit(solution)/shard_map/chain/pallas_call | solution.py:85
  103.4 1.0 copy-done
  104.4 0.0 all-to-all-done.3
  104.4 0.8 slice.37
  105.2 0.1 copy.23
  105.3 1.8 %convert_multiply_fusion = f32[16,384,128]{2,1,0:T(8,128)S(1)} fusion(f16[16,400,128]{2,1,0:T(8,128)(2,1)} %all-to-all-done.3, f32[16]{0:T(128)S(1)} %exponential_bitcast_fusion), kind=kLoop, calls=%fused_computation | loop fusion | flops 1572864 | bytes 4718656 | tf_op jit(solution)/shard_map/mul | solution.py:194
  107.1 0.0 all-gather.3.cloned.1.call-done
  107.1 0.0 copy-start.1
  107.1 1.3 copy-done.1
  108.4 11.9 %finish.1 = (f32[8,6,128,128]{3,2,1,0:T(8,128)}, f32[8,8,128,128]{3,2,1,0:T(8,128)}) custom-call(s32[2]{0:T(128)S(1)} %pad_add_fusion.place_ref, f32[8,8,128,128]{3,2,1,0:T(8,128)} %bitcast.29, f32[16,6,8,8,128]{4,3,2,1,0:T(8,128)S(1)} %bitcast.26, f32[16,8,128,128]{3,2,1,0:T(8,128)} %bitcast.27, bf16[768,768]{1,0:T(8,128)(2,1)S(1)} %copy-done.1, ...), custom_call_target="tpu_custom_call" | custom-call | tf_op jit(solution)/shard_map/finish/pallas_call | solution.py:152
  (6 shorter events, 0.1 us)
Async XLA Ops:
  7.2 100.0 %all-gather.3.cloned.1.call-start = ((), (), s32[]{:S(2)}) async-start(), calls=%async_computation.4 | async-start | bytes 8912896 | tf_op jit(solution)/shard_map/all_gather | solution.py:201
  66.5 5.7 %collective-permute-start = (f32[16,12,8,128]{3,2,1,0:T(8,128)S(1)}, f32[16,12,8,128]{3,2,1,0:T(8,128)S(1)}, u32[]{:S(2)}, u32[]{:S(2)}) collective-permute-start(f32[16,12,8,128]{3,2,1,0:T(8,128)S(1)} %all_to_all.26.mine_ref), channel_id=1, source_target_pairs={{0,16},{16,0},{32,48},{48,32},{64,80},{80,64},{96,112},{112,96},{1... | collective-permute-start | bytes 2359304 | tf_op jit(solution)/shard_map/ppermute | solution.py:208
  73.5 30.8 %all-to-all-start.3 = ((f16[16,400,128]{2,1,0:T(8,128)(2,1)}), f16[16,400,128]{2,1,0:T(8,128)(2,1)}, u32[]{:S(2)}, u32[]{:S(2)}) async-start(f16[16,400,128]{2,1,0:T(8,128)(2,1)} %broadcast_in_dim.22), calls=%async_computation.3 | async-start | bytes 3276800 | tf_op jit(solution)/shard_map/all_to_all | solution.py:211
  103.4 1.0 copy-start
  107.1 1.3 %copy-start.1 = (bf16[768,768]{1,0:T(8,128)(2,1)S(1)}, bf16[768,768]{1,0:T(8,128)(2,1)}, u32[]{:S(2)}) copy-start(bf16[768,768]{1,0:T(8,128)(2,1)} %copy-done) | copy-start | bytes 3538948
Sparse Core Ops, SparseCore 0:
  9.8 64.3 all-gather.2

commit v3 on v2

v3 whole, which is shorter than its diff:
```python
import jax
import jax.numpy as jnp
from jax import lax
from jax.experimental import pallas as pl
from jax.experimental.pallas import tpu as pltpu
from jax.sharding import PartitionSpec as P

STEPS = 6
NB = 128
LT = 8
SB = 32
HALF = 12
SHIFT = 13.0


def split2(x):
    hi = x.astype(jnp.bfloat16)
    lo = (x - hi.astype(jnp.float32)).astype(jnp.bfloat16)
    return hi, lo

def chain_kernel(place_ref, mine_ref, other_ref, top_hbm, ub_ref, linv_ref, q_ref, logdet_ref, w_ref, d_ref, top_ref, sem):
    tops = pltpu.make_async_copy(top_hbm.at[pl.ds(0, STEPS)], top_ref, sem)
    tops.start()
    col = place_ref[1]
    core = lax.rem(place_ref[0], 2)
    for n in range(HALF):
        d_ref[core, n] = mine_ref[:, n].reshape(NB, NB)
        d_ref[1 - core, n] = other_ref[:, n].reshape(NB, NB)
    ub_ref[...] = jnp.zeros_like(ub_ref)
    q_ref[...] = jnp.zeros_like(q_ref)
    eye = (lax.broadcasted_iota(jnp.int32, (NB, NB), 0) == lax.broadcasted_iota(jnp.int32, (NB, NB), 1)).astype(jnp.float32)
    rows8 = lax.broadcasted_iota(jnp.int32, (8, NB), 0)
    ri = lax.broadcasted_iota(jnp.int32, (NB, NB), 0)
    ci = lax.broadcasted_iota(jnp.int32, (NB, NB), 1)

    def columns(k):
        kk = pl.multiple_of(k * NB, NB)
        lhi, llo = split2(linv_ref[k])
        x = jnp.concatenate([top_ref[k, m] for m in range(LT)], axis=1)
        x = x - lax.dot_general(ub_ref[:, pl.ds(kk, NB)], q_ref[...], (((0,), (0,)), ((), ())),
                                preferred_element_type=jnp.float32)
        xhi, xlo = split2(x)
        q = jnp.dot(jnp.concatenate([lhi, lhi, llo], axis=1), jnp.concatenate([xhi, xlo, xhi], axis=0),
                    preferred_element_type=jnp.float32)
        keep = jnp.where(col == k, ci - ri, col - k) >= 0
        q_ref[pl.ds(kk, NB), :NB] = jnp.where(keep, q[:, :NB], 0.0).astype(jnp.bfloat16)
        q_ref[pl.ds(kk, NB), NB:] = q[:, NB:].astype(jnp.bfloat16)

    def step(k, logs):
        kk = pl.multiple_of(k * NB, NB)
        left = ub_ref[:, pl.ds(kk, NB)]
        for t in range(STEPS):
            j = lax.rem(k + t, STEPS)
            jj = pl.multiple_of(j * NB, NB)
            low, high = jnp.minimum(k, j), jnp.maximum(k, j)
            pair = low // 2
            place = pair * STEPS - pair * (pair - 1) + high - 2 * pair
            upd = lax.dot_general(left, ub_ref[:, pl.ds(jj, NB)], (((0,), (0,)), ((), ())), preferred_element_type=jnp.float32)
            w_ref[:, t * NB:(t + 1) * NB] = d_ref[lax.rem(low, 2), place] - upd
        w_ref[:, STEPS * NB:] = eye
        if not isinstance(k, int):
            columns(k - 1)
        wide = (0, STEPS)
        for s in range(NB // SB):
            r0 = s * SB
            nb = SB // 8
            R = [[w_ref[r0 + 8 * b:r0 + 8 * b + 8, t * NB:(t + 1) * NB] for b in range(nb)] for t in wide]
            cols = [{b: jnp.broadcast_to(R[0][b][:, r0 + q:r0 + q + 1], (8, NB)) for b in range(q // 8, nb)} for q in range(SB)]
            for p in range(SB):
                pb, pr = p // 8, p % 8
                inv = lax.rsqrt(jnp.broadcast_to(cols[p][pb][pr:pr + 1, :], (8, NB)))
                l = {b: cols[p][b] * inv for b in range(pb, nb)}
                for q in range(p + 1, SB):
                    m = jnp.broadcast_to(l[q // 8][q % 8:q % 8 + 1, :], (8, NB))
                    for b in range(q // 8, nb):
                        cols[q][b] = cols[q][b] - l[b] * m
                for t in range(2):
                    u = jnp.broadcast_to(R[t][pb][pr:pr + 1, :], (8, NB)) * inv
                    if pr < 7:
                        R[t][pb] = jnp.where(rows8 == pr, u, R[t][pb] - jnp.where(rows8 > pr, l[pb], 0.0) * u)
                    else:
                        R[t][pb] = jnp.where(rows8 == pr, u, R[t][pb])
                    for b in range(pb + 1, nb):
                        R[t][b] = R[t][b] - l[b] * u
            R = [jnp.concatenate(x, axis=0) for x in R]
            for t in range(2):
                w_ref[r0:r0 + SB, wide[t] * NB:(wide[t] + 1) * NB] = R[t]
            if s < NB // SB - 1:
                X = jnp.concatenate(R, axis=1)
                xhi, xlo = split2(X)
                r1 = r0 + SB
                lh, ll = xhi[:, :NB], xlo[:, :NB]
                L = jnp.concatenate([lh, lh, ll], axis=0).T
                Rr = jnp.concatenate([xhi, xlo, xhi], axis=0)
                cuts = [(r1, NB)]
                for lo_, hi_ in cuts:
                    if lo_ < hi_:
                        upd = jnp.dot(L[lo_:hi_], Rr, preferred_element_type=jnp.float32)
                        for t in range(2):
                            sl = slice(wide[t] * NB, (wide[t] + 1) * NB)
                            w_ref[lo_:hi_, sl] = w_ref[lo_:hi_, sl] - upd[:, t * NB:(t + 1) * NB]
        lhi, llo = split2(w_ref[:, STEPS * NB:])
        shi, slo = split2(w_ref[:, NB:STEPS * NB])
        w_ref[:, NB:STEPS * NB] = jnp.dot(jnp.concatenate([lhi, lhi, llo], axis=1), jnp.concatenate([shi, slo, shi], axis=0), preferred_element_type=jnp.float32)
        tri = lax.broadcasted_iota(jnp.int32, (NB, NB), 0) <= lax.broadcasted_iota(jnp.int32, (NB, NB), 1)
        for t in range(STEPS):
            j = lax.rem(k + t, STEPS)
            jj = pl.multiple_of(j * NB, NB)
            keep = k + t < STEPS
            x = w_ref[:, t * NB:(t + 1) * NB]
            if t == 0:
                x = jnp.where(tri, x, 0.0)
                logs = logs + jnp.sum(jnp.log(jnp.sum(x * eye, axis=0, keepdims=True)), axis=1, keepdims=True)
            else:
                x = jnp.where(keep, x, 0.0)
            ub_ref[pl.ds(kk, NB), pl.ds(jj, NB)] = x.astype(jnp.bfloat16)
        linv_ref[k] = w_ref[:, STEPS * NB:]
        return logs

    logs = step(0, jnp.zeros((1, 1), jnp.float32))
    tops.wait()
    logs = lax.fori_loop(1, STEPS, step, logs)
    columns(STEPS - 1)
    logdet_ref[...] = logs * (2.0 / (STEPS * NB))

def chain(place, mine, other, top):
    return pl.pallas_call(
        chain_kernel,
        out_shape=(jax.ShapeDtypeStruct((STEPS * NB, STEPS * NB), jnp.bfloat16),
                   jax.ShapeDtypeStruct((STEPS, NB, NB), jnp.float32),
                   jax.ShapeDtypeStruct((STEPS * NB, LT * NB), jnp.bfloat16),
                   jax.ShapeDtypeStruct((1, 1), jnp.float32)),
        in_specs=[pl.BlockSpec(memory_space=pltpu.SMEM)] + [pl.BlockSpec(memory_space=pltpu.VMEM)] * 2 + [pl.BlockSpec(memory_space=pltpu.HBM)],
        out_specs=(pl.BlockSpec(memory_space=pltpu.VMEM),) * 4,
        scratch_shapes=[pltpu.VMEM((NB, (STEPS + 1) * NB), jnp.float32), pltpu.VMEM((2, HALF, NB, NB), jnp.float32),
                        pltpu.VMEM((STEPS, LT, NB, NB), jnp.float32), pltpu.SemaphoreType.DMA],
        compiler_params=pltpu.CompilerParams(vmem_limit_bytes=50 * 2**20),
        cost_estimate=pl.CostEstimate(flops=30_000_000_000, bytes_accessed=4 * 2**20, transcendentals=0),
        name="chain",
    )(place, mine, other, top)


def finish_kernel(place_ref, a_hbm, rp_ref, q_ref, ub_ref, linv_ref, pf_hbm, tr_hbm, a_ref, p_ref, b_ref, in_sem, p_sem, t_sem):
    row = place_ref[0]
    pairs = LT // 2
    loads = [pltpu.make_async_copy(a_hbm.at[:, pl.ds(2 * n, 2)], a_ref.at[n], in_sem.at[n]) for n in range(pairs)]
    for copy in loads:
        copy.start()
    ri = lax.broadcasted_iota(jnp.int32, (NB, NB), 0)
    ci = lax.broadcasted_iota(jnp.int32, (NB, NB), 1)
    scale = jnp.exp2(rp_ref[:, STEPS * LT * 8:STEPS * LT * 8 + 8] - SHIFT).reshape(NB, NB)
    stores = []
    later = None
    for k in range(STEPS):
        lhi, llo = split2(linv_ref[k])
        tiles = [rp_ref[:, (k * LT + l) * 8:(k * LT + l + 1) * 8].reshape(NB, NB) * scale for l in range(LT)]
        s = jnp.concatenate(tiles, axis=0)
        if k % 2 == 0:
            if k:
                both = jnp.dot(b_ref[:, :k * NB], ub_ref[:k * NB, k * NB:(k + 2) * NB], preferred_element_type=jnp.float32)
                s = s - both[:, :NB]
                later = both[:, NB:]
        else:
            s = s - jnp.dot(b_ref[:, (k - 1) * NB:k * NB], ub_ref[(k - 1) * NB:k * NB, k * NB:(k + 1) * NB],
                            preferred_element_type=jnp.float32)
            if k > 1:
                s = s - later
        shi, slo = split2(s)
        zero = jnp.zeros_like(llo)
        weights = jnp.concatenate([jnp.concatenate([lhi, lhi], axis=1), jnp.concatenate([llo, zero], axis=1)], axis=0)
        p = lax.dot_general(jnp.concatenate([shi, slo], axis=1), weights, (((1,), (1,)), ((), ())),
                            preferred_element_type=jnp.float32)
        p = p[:, :NB] + p[:, NB:]
        keep = jnp.where(row == k, ri - ci, row - k) >= 0
        first = jnp.where(keep, p[:NB], 0.0)
        p_ref[0, k] = first
        for l in range(1, LT):
            p_ref[l, k] = p[l * NB:(l + 1) * NB]
        b_ref[:NB, k * NB:(k + 1) * NB] = first.astype(jnp.bfloat16)
        b_ref[NB:, k * NB:(k + 1) * NB] = p[NB:].astype(jnp.bfloat16)
        store = pltpu.make_async_copy(p_ref.at[:, k], pf_hbm.at[:, k], p_sem.at[k])
        store.start()
        stores.append(store)
    for n in range(pairs):
        loads[n].wait()
        upd = jnp.dot(b_ref[...], q_ref[:, 2 * n * NB:2 * (n + 1) * NB], preferred_element_type=jnp.float32)
        for l in range(LT):
            for m in range(2):
                a_ref[n, l, m] = a_ref[n, l, m] - upd[l * NB:(l + 1) * NB, m * NB:(m + 1) * NB]
        store = pltpu.make_async_copy(a_ref.at[n], tr_hbm.at[:, pl.ds(2 * n, 2)], t_sem.at[n])
        store.start()
        stores.append(store)
    for store in stores:
        store.wait()


def finish(place, a, rp, q, ub, linv):
    vm = pl.BlockSpec(memory_space=pltpu.VMEM)
    hb = pl.BlockSpec(memory_space=pltpu.HBM)
    return pl.pallas_call(
        finish_kernel,
        out_shape=(jax.ShapeDtypeStruct((LT, STEPS, NB, NB), jnp.float32),
                   jax.ShapeDtypeStruct((LT, LT, NB, NB), jnp.float32)),
        in_specs=[pl.BlockSpec(memory_space=pltpu.SMEM), hb, vm, vm, vm, vm],
        out_specs=(hb, hb),
        scratch_shapes=[pltpu.VMEM((LT // 2, LT, 2, NB, NB), jnp.float32), pltpu.VMEM((LT, STEPS, NB, NB), jnp.float32),
                        pltpu.VMEM((LT * NB, STEPS * NB), jnp.bfloat16), pltpu.SemaphoreType.DMA((LT // 2,)),
                        pltpu.SemaphoreType.DMA((STEPS,)), pltpu.SemaphoreType.DMA((LT // 2,))],
        compiler_params=pltpu.CompilerParams(vmem_limit_bytes=44 * 2**20),
        cost_estimate=pl.CostEstimate(flops=4_000_000_000, bytes_accessed=14 * 2**20, transcendentals=0),
        name="finish",
    )(place, a, rp, q, ub, linv)


def spread_kernel(x_ref, o_ref):
    tiles = [x_ref[p, q] for p in range(STEPS // 2) for q in range(2 * p, STEPS)]
    for j in range(16):
        for n, tile in enumerate(tiles):
            o_ref[j, n] = tile


def spread_half(x):
    return pl.pallas_call(
        spread_kernel,
        out_shape=jax.ShapeDtypeStruct((16, HALF, 8, NB), jnp.float32),
        in_specs=[pl.BlockSpec(memory_space=pltpu.VMEM)],
        out_specs=pl.BlockSpec(memory_space=pltpu.VMEM),
        compiler_params=pltpu.CompilerParams(vmem_limit_bytes=4 * 2**20),
        name="spread",
    )(x)


def packed(x):
    top = jnp.maximum(jnp.max(jnp.abs(x)), 1e-30)
    power = jnp.floor(jnp.log2(top))
    body = (x * jnp.exp2(SHIFT - power)).astype(jnp.float16)
    return jnp.concatenate([body, jnp.full((16, NB), power, jnp.float16)], axis=0)


def shards(covariance):
    matrix = covariance[:, 0, :, 0]
    row = lax.axis_index("row")
    place = jnp.stack([row, lax.axis_index("col")]).astype(jnp.int32)
    across = lax.all_gather(matrix[0], "row", axis=0, tiled=False)
    first = matrix[:, 0].reshape(LT, 16, 8, NB).transpose(1, 0, 2, 3).reshape(16 * LT * 8, NB)
    slabs = lax.all_to_all(first, "col", 0, 0, tiled=True).reshape(16, LT, 8, NB)[:STEPS]
    sent = jnp.broadcast_to(slabs[None, :, 0], (8, STEPS, 8, NB))
    groups = [[2 * z + c for z in range(8)] for c in range(2)]
    lead = lax.all_to_all(sent, "row", 0, 0, tiled=True, axis_index_groups=groups)
    mine = lax.all_to_all(spread_half(lead), "col", 0, 0, tiled=True)
    other = lax.ppermute(mine, "row", [(i, i ^ 1) for i in range(16)])
    half = packed(slabs.reshape(STEPS * LT * 8, NB))
    half, mine = lax.optimization_barrier((jnp.broadcast_to(half[None], (16,) + half.shape), mine))
    down = lax.all_to_all(half, "col", 0, 0, tiled=True)
    ub, linv, q, logdet = chain(place, mine, other, across)
    down, q = lax.optimization_barrier((down, q))
    panel, trailing = finish(place, matrix, down.astype(jnp.float32), q, ub, linv)
    return panel[:, None], trailing[:, None, :, None], logdet[0, 0]


def solution(mesh):
    in_specs = (P(None, "row", None, "col", None, None),)
    out_specs = (P(None, "row", None, None, None), P(None, "row", None, "col", None, None), P())
    return jax.shard_map(shards, mesh=mesh, in_specs=in_specs, out_specs=out_specs, check_vma=False)
```

time: 128 us -> 120 us (0.938)
  Pallas kernels: 39.2 us -> 33.8 us
  local copies, waits for them, and re-layouts: 7.55 us -> 4.39 us
  waiting for transfers between devices: 1.85 us -> 3.35 us
    all_to_all x1, waiting for transfers between devices: 0.01 us -> 2.57 us  [shards(): down = lax.all_to_all(half, 'col', 0, 0, tiled=True)]
    pallas_call x1, Pallas kernels: 11.9 us -> 9.44 us  [finish(): pl.pallas_call(finish_kernel, out_shape=(jax.ShapeDtypeStruct((LT, STEPS,...]
    unnamed x5 -> x2, local copies, waits for them, and re-layouts: 2.38 us -> 0.01 us
    pallas_call x1, Pallas kernels: 1.92 us -> 0.07 us  [spread_half(): pl.pallas_call(spread_kernel, out_shape=jax.ShapeDtypeStruct((16, HALF, 8...]
    mul x2 -> x0, other arithmetic: 1.83 us -> none  [unpacked(): return x[:, :-16].astype(jnp.float32) * jnp.exp2(power - SHIFT)]
    ppermute x1, waiting for transfers between devices: 1.81 us -> 0.01 us  [shards(): other = lax.ppermute(mine, 'row', [(i, i ^ 1) for i in range(16)])]
    convert_element_type x0 -> x1, other arithmetic: none -> 1.64 us  [shards(): down.astype(jnp.float32)]
  transfers between devices with their start and end apart: 3 -> 3, of which waited for: 1 -> 2; matrix products, arithmetic and copies ran while one was open for 5% -> 3% of each run, Pallas kernels for 21% -> 20%
where the time goes in v3:
time: 120 us
  blocking collectives  52.8 us (44%)
  Pallas kernels  33.8 us (28%)
  between operations  14.9 us (12%)
  starting transfers between devices  8.04 us (7%)
  local copies, waits for them, and re-layouts  4.39 us (4%)
  waiting for transfers between devices  3.35 us (3%)
  other arithmetic  2.36 us (2%)
    pallas_call x1, Pallas kernels, chain(): pl.pallas_call(chain_kernel, out_shape=(jax.ShapeDtypeStruct((STEPS * NB,...  24.3 us
    all_to_all x1, blocking collectives, shards(): lax.all_to_all(sent, 'row', 0, 0, tiled=True, axis_index_groups=groups)  19.8 us
    all_to_all x1, blocking collectives, shards(): lax.all_to_all(first, 'col', 0, 0, tiled=True).reshape(16, LT, 8, NB)  17.9 us
    all_to_all x1, blocking collectives, shards(): mine = lax.all_to_all(spread_half(lead), 'col', 0, 0, tiled=True)  15.1 us
    pallas_call x1, Pallas kernels, finish(): pl.pallas_call(finish_kernel, out_shape=(jax.ShapeDtypeStruct((LT, STEPS,...  9.44 us
    all_to_all x1, starting transfers between devices, shards(): down = lax.all_to_all(half, 'col', 0, 0, tiled=True)  4.4 us
    ppermute x1, starting transfers between devices, shards(): other = lax.ppermute(mine, 'row', [(i, i ^ 1) for i in range(16)])  3.6 us
    all_to_all x1, waiting for transfers between devices, shards(): down = lax.all_to_all(half, 'col', 0, 0, tiled=True)  2.57 us
  transfers between devices with their start and end apart: 3, of which 2 were waited for; matrix products, arithmetic and copies ran while one was open for 3% of the time, Pallas kernels for 20%

profile of v3, /device:TPU:1, one launch (start us, length us, event | category | flops | bytes accessed | tf_op | source)
XLA Modules:
  0.0 119.6 jit_solution(10432256395280164639)
XLA Ops:
  7.2 0.0 all-gather.3.cloned.1.call-start
  7.2 1.9 %slice.23 = f32[1,1,8,1,128,128]{5,4,3,2,1,0:T(8,128)} slice(f32[8,1,8,1,128,128]{5,4,3,2,1,0:T(8,128)} %param.1), slice={[0:1], [0:1], [0:8], [0:1], [0:128], [0:128]} | slice | bytes 1048576 | tf_op jit(solution)/shard_map/slice | solution.py:244
  9.1 0.0 all-gather.3.cloned.1.call-update
  9.1 1.1 copy_bitcast_fusion
  10.2 17.9 %all_to_all.24 = f32[16,64,128]{2,1,0:T(8,128)S(1)} all-to-all(f32[16,64,128]{2,1,0:T(8,128)S(1)} %copy_bitcast_fusion), channel_id=1, replica_groups=mesh['row'=16,'col'=16] {'col'}, dimensions={0} | all-to-all | bytes 1048576 | tf_op jit(solution)/shard_map/all_to_all | solution.py:246
  28.1 0.6 abs_reduce_fusion
  29.5 19.8 %all_to_all.25.x_ref = f32[8,6,8,128]{3,2,1,0:T(8,128)S(1)} all-to-all(f32[8,6,8,128]{3,2,1,0:T(8,128)S(1)} %broadcast_in_dim.22), channel_id=1, replica_groups={{0,32,64,96,128,160,192,224},{16,48,80,112,144,176,208,240},{1,33,65,97..., dimensions={0} | all-to-all | bytes 393216 | tf_op jit(solution)/shard_map/all_to_all | solution.py:249
  49.3 0.1 spread.1
  49.4 15.1 %all_to_all.26.mine_ref = f32[16,12,8,128]{3,2,1,0:T(8,128)S(1)} all-to-all(f32[16,12,8,128]{3,2,1,0:T(8,128)S(1)} %spread.1), channel_id=1, replica_groups=mesh['row'=16,'col'=16] {'col'}, dimensions={0} | all-to-all | bytes 1572864 | tf_op jit(solution)/shard_map/all_to_all | solution.py:250
  64.5 3.6 %collective-permute-start = (f32[16,12,8,128]{3,2,1,0:T(8,128)S(1)}, f32[16,12,8,128]{3,2,1,0:T(8,128)S(1)}, u32[]{:S(2)}, u32[]{:S(2)}) collective-permute-start(f32[16,12,8,128]{3,2,1,0:T(8,128)S(1)} %all_to_all.26.mine_ref), channel_id=1, source_target_pairs={{0,16},{16,0},{32,48},{48,32},{64,80},{80,64},{96,112},{112,96},{1... | collective-permute-start | bytes 2359304 | tf_op jit(solution)/shard_map/ppermute | solution.py:251
  68.1 0.1 pad_add_fusion.place_ref
  68.2 1.4 %broadcast_in_dim.20 = f16[16,400,128]{2,1,0:T(8,128)(2,1)} broadcast(f16[400,128]{1,0:T(8,128)(2,1)S(1)} %concatenate.3), dimensions={1,2} | broadcast | bytes 1740800 | tf_op jit(solution)/shard_map/broadcast_in_dim | solution.py:253
  69.6 4.4 %all-to-all-start.3 = ((f16[16,400,128]{2,1,0:T(8,128)(2,1)}), f16[16,400,128]{2,1,0:T(8,128)(2,1)}, u32[]{:S(2)}, u32[]{:S(2)}) async-start(f16[16,400,128]{2,1,0:T(8,128)(2,1)} %broadcast_in_dim.20), calls=%async_computation.3 | async-start | bytes 3276800 | tf_op jit(solution)/shard_map/all_to_all | solution.py:254
  74.0 0.0 collective-permute-done.other_ref
  74.0 0.8 all-gather.3.cloned.1.call-done
  74.8 24.3 %chain.1 = (bf16[768,768]{1,0:T(8,128)(2,1)S(1)}, f32[6,128,128]{2,1,0:T(8,128)S(1)}, bf16[768,1024]{1,0:T(8,128)(2,1)}, f32[1,1]{1,0:T(1,128)}) custom-call(s32[2]{0:T(128)S(1)} %pad_add_fusion.place_ref, f32[16,12,8,128]{3,2,1,0:T(8,128)S(1)} %all_to_all.26.mine_ref, f32[16,12,8,128]{3,2,1,0:T(8,128)S(1)} %collective-permute-done.other_ref, ...), custom_call_target="tpu_custom_call" | custom-call | flops 30000001024 | bytes 4194304 | tf_op jit(solution)/shard_map/chain/pallas_call | solution.py:127
  99.1 0.0 copy-start
  99.1 2.6 %all-to-all-done.3 = f16[16,400,128]{2,1,0:T(8,128)(2,1)} async-done(((f16[16,400,128]{2,1,0:T(8,128)(2,1)}), f16[16,400,128]{2,1,0:T(8,128)(2,1)}, u32[]{:S(2)}, u32[]{:S(2)}) %all-to-all-start.3) | async-done | bytes 1638432 | tf_op jit(solution)/shard_map/all_to_all | solution.py:254
  101.6 1.6 %convert_element_type.15.rp_ref = f32[16,400,128]{2,1,0:T(8,128)S(1)} convert(f16[16,400,128]{2,1,0:T(8,128)(2,1)} %all-to-all-done.3) | non-fusion elementwise | flops 819200 | bytes 4915200 | tf_op jit(solution)/shard_map/convert_element_type | solution.py:257
  103.3 0.0 copy-done
  103.3 9.4 %finish.1 = (f32[8,6,128,128]{3,2,1,0:T(8,128)}, f32[8,8,128,128]{3,2,1,0:T(8,128)}) custom-call(s32[2]{0:T(128)S(1)} %pad_add_fusion.place_ref, f32[8,8,128,128]{3,2,1,0:T(8,128)} %bitcast.25, f32[16,400,128]{2,1,0:T(8,128)S(1)} %convert_element_type.15.rp_ref, bf16[768,1024]{1,0:T(8,128)(2,1)S(1)} %copy-done, ...), custom_call_target="tpu_custom_call" | custom-call | flops 4000000000 | bytes 14680064 | tf_op jit(solution)/shard_map/finish/pallas_call | solution.py:200
  (4 shorter events, 0.1 us)
Async XLA Ops:
  7.2 67.6 %all-gather.3.cloned.1.call-start = ((), (), s32[]{:S(2)}) async-start(), calls=%async_computation.4 | async-start | bytes 8912896 | tf_op jit(solution)/shard_map/all_gather | solution.py:244
  64.5 9.5 %collective-permute-start = (f32[16,12,8,128]{3,2,1,0:T(8,128)S(1)}, f32[16,12,8,128]{3,2,1,0:T(8,128)S(1)}, u32[]{:S(2)}, u32[]{:S(2)}) collective-permute-start(f32[16,12,8,128]{3,2,1,0:T(8,128)S(1)} %all_to_all.26.mine_ref), channel_id=1, source_target_pairs={{0,16},{16,0},{32,48},{48,32},{64,80},{80,64},{96,112},{112,96},{1... | collective-permute-start | bytes 2359304 | tf_op jit(solution)/shard_map/ppermute | solution.py:251
  69.6 32.0 %all-to-all-start.3 = ((f16[16,400,128]{2,1,0:T(8,128)(2,1)}), f16[16,400,128]{2,1,0:T(8,128)(2,1)}, u32[]{:S(2)}, u32[]{:S(2)}) async-start(f16[16,400,128]{2,1,0:T(8,128)(2,1)} %broadcast_in_dim.20), calls=%async_computation.3 | async-start | bytes 3276800 | tf_op jit(solution)/shard_map/all_to_all | solution.py:254
  99.1 4.2 %copy-start = (bf16[768,1024]{1,0:T(8,128)(2,1)S(1)}, bf16[768,1024]{1,0:T(8,128)(2,1)}, u32[]{:S(2)}) copy-start(bf16[768,1024]{1,0:T(8,128)(2,1)} %get-tuple-element.17.q_ref) | copy-start | bytes 4718596
Sparse Core Ops, SparseCore 0:
  10.4 64.3 all-gather.2

commit v4 on v3

--- a/solution.py
+++ b/solution.py
@@ -181,15 +181,20 @@
         store = pltpu.make_async_copy(p_ref.at[:, k], pf_hbm.at[:, k], p_sem.at[k])
         store.start()
         stores.append(store)
-    for n in range(pairs):
-        loads[n].wait()
-        upd = jnp.dot(b_ref[...], q_ref[:, 2 * n * NB:2 * (n + 1) * NB], preferred_element_type=jnp.float32)
-        for l in range(LT):
-            for m in range(2):
-                a_ref[n, l, m] = a_ref[n, l, m] - upd[l * NB:(l + 1) * NB, m * NB:(m + 1) * NB]
-        store = pltpu.make_async_copy(a_ref.at[n], tr_hbm.at[:, pl.ds(2 * n, 2)], t_sem.at[n])
-        store.start()
-        stores.append(store)
+        if k % 2 == 0:
+            continue
+        for n in range(pairs):
+            if k == 1:
+                loads[n].wait()
+            upd = jnp.dot(b_ref[:, (k - 1) * NB:(k + 1) * NB], q_ref[(k - 1) * NB:(k + 1) * NB, 2 * n * NB:2 * (n + 1) * NB],
+                          preferred_element_type=jnp.float32)
+            for l in range(LT):
+                for m in range(2):
+                    a_ref[n, l, m] = a_ref[n, l, m] - upd[l * NB:(l + 1) * NB, m * NB:(m + 1) * NB]
+            if k == STEPS - 1:
+                store = pltpu.make_async_copy(a_ref.at[n], tr_hbm.at[:, pl.ds(2 * n, 2)], t_sem.at[n])
+                store.start()
+                stores.append(store)
     for store in stores:
         store.wait()
 
@@ -212,6 +217,28 @@
     )(place, a, rp, q, ub, linv)
 
 
+def cut_kernel(a_hbm, top_hbm, first_ref, top_sem, sem):
+    top = pltpu.make_async_copy(a_hbm.at[0], top_hbm, top_sem)
+    top.start()
+    cuts = [pltpu.make_async_copy(a_hbm.at[l, 0], first_ref.at[:, l], sem.at[l]) for l in range(LT)]
+    for copy in cuts:
+        copy.start()
+    for copy in cuts + [top]:
+        copy.wait()
+
+
+def cut(a):
+    return pl.pallas_call(
+        cut_kernel,
+        out_shape=(jax.ShapeDtypeStruct((LT, 16, 8, NB), jnp.float32), jax.ShapeDtypeStruct((16, LT, 8, NB), jnp.float32)),
+        in_specs=[pl.BlockSpec(memory_space=pltpu.HBM)],
+        out_specs=(pl.BlockSpec(memory_space=pltpu.HBM), pl.BlockSpec(memory_space=pltpu.VMEM)),
+        scratch_shapes=[pltpu.SemaphoreType.DMA, pltpu.SemaphoreType.DMA((LT,))],
+        compiler_params=pltpu.CompilerParams(vmem_limit_bytes=58 * 2**20),
+        name="cut",
+    )(a)
+
+
 def spread_kernel(x_ref, o_ref):
     tiles = [x_ref[p, q] for p in range(STEPS // 2) for q in range(2 * p, STEPS)]
     for j in range(16):
@@ -241,9 +268,9 @@
     matrix = covariance[:, 0, :, 0]
     row = lax.axis_index("row")
     place = jnp.stack([row, lax.axis_index("col")]).astype(jnp.int32)
-    across = lax.all_gather(matrix[0], "row", axis=0, tiled=False)
-    first = matrix[:, 0].reshape(LT, 16, 8, NB).transpose(1, 0, 2, 3).reshape(16 * LT * 8, NB)
-    slabs = lax.all_to_all(first, "col", 0, 0, tiled=True).reshape(16, LT, 8, NB)[:STEPS]
+    top, first = cut(matrix.reshape(LT, LT, 16, 8, NB))
+    across = lax.all_gather(top.reshape(LT, NB, NB), "row", axis=0, tiled=False)
+    slabs = lax.all_to_all(first.reshape(16 * LT * 8, NB), "col", 0, 0, tiled=True).reshape(16, LT, 8, NB)[:STEPS]
     sent = jnp.broadcast_to(slabs[None, :, 0], (8, STEPS, 8, NB))
     groups = [[2 * z + c for z in range(8)] for c in range(2)]
     lead = lax.all_to_all(sent, "row", 0, 0, tiled=True, axis_index_groups=groups)

time: 120 us -> 134 us (1.12)
  Pallas kernels: 33.8 us -> 50.5 us
  local copies, waits for them, and re-layouts: 4.39 us -> 1.43 us
    pallas_call x0 -> x1, Pallas kernels: none -> 17.9 us  [cut(): pl.pallas_call(cut_kernel, out_shape=(jax.ShapeDtypeStruct((LT, 16, 8, NB...]
    slice x1 -> x0, local copies, waits for them, and re-layouts: 1.87 us -> none  [shards(): across = lax.all_gather(matrix[0], 'row', axis=0, tiled=False)]
  transfers between devices with their start and end apart: 3 -> 3, of which waited for: 2 -> 2; matrix products, arithmetic and copies ran while one was open for 3% -> 2% of each run, Pallas kernels for 20% -> 18%
where the time goes in v4:
time: 134 us
  blocking collectives  53 us (40%)
  Pallas kernels  50.5 us (38%)
  between operations  14.9 us (11%)
  starting transfers between devices  8.04 us (6%)
  waiting for transfers between devices  3.32 us (2%)
  other arithmetic  2.36 us (2%)
  local copies, waits for them, and re-layouts  1.43 us (1%)
    pallas_call x1, Pallas kernels, chain(): pl.pallas_call(chain_kernel, out_shape=(jax.ShapeDtypeStruct((STEPS * NB,...  24.3 us
    all_to_all x1, blocking collectives, shards(): lax.all_to_all(sent, 'row', 0, 0, tiled=True, axis_index_groups=groups)  19.8 us
    all_to_all x1, blocking collectives, shards(): lax.all_to_all(first.reshape(16 * LT * 8, NB), 'col', 0, 0, tiled=True)  18.1 us
    pallas_call x1, Pallas kernels, cut(): pl.pallas_call(cut_kernel, out_shape=(jax.ShapeDtypeStruct((LT, 16, 8, NB...  17.9 us
    all_to_all x1, blocking collectives, shards(): mine = lax.all_to_all(spread_half(lead), 'col', 0, 0, tiled=True)  15.1 us
    pallas_call x1, Pallas kernels, finish(): pl.pallas_call(finish_kernel, out_shape=(jax.ShapeDtypeStruct((LT, STEPS,...  8.29 us
    all_to_all x1, starting transfers between devices, shards(): down = lax.all_to_all(half, 'col', 0, 0, tiled=True)  4.4 us
    ppermute x1, starting transfers between devices, shards(): other = lax.ppermute(mine, 'row', [(i, i ^ 1) for i in range(16)])  3.6 us
  transfers between devices with their start and end apart: 3, of which 2 were waited for; matrix products, arithmetic and copies ran while one was open for 2% of the time, Pallas kernels for 18%

profile of v4, /device:TPU:1, one launch (start us, length us, event | category | flops | bytes accessed | tf_op | source)
XLA Modules:
  0.0 133.6 jit_solution(2858537808045674789)
XLA Ops:
  7.2 0.0 all-gather.2.cloned.1.call-start
  7.2 17.9 %cut.1 = (f32[8,16,8,128]{3,2,1,0:T(8,128)}, f32[16,8,8,128]{3,2,1,0:T(8,128)}) custom-call(f32[8,8,16,8,128]{4,3,2,1,0:T(8,128)} %bitcast.18), custom_call_target="tpu_custom_call" | custom-call | tf_op jit(solution)/shard_map/cut/pallas_call | solution.py:231
  25.1 0.0 all-gather.2.cloned.1.call-update
  25.1 18.1 %all_to_all.24 = f32[16,64,128]{2,1,0:T(8,128)S(1)} all-to-all(f32[16,64,128]{2,1,0:T(8,128)} %bitcast.21), channel_id=1, replica_groups=mesh['row'=16,'col'=16] {'col'}, dimensions={0} | all-to-all | bytes 1048576 | tf_op jit(solution)/shard_map/all_to_all | solution.py:273
  43.2 0.6 abs_reduce_fusion
  44.6 19.8 %all_to_all.25.x_ref = f32[8,6,8,128]{3,2,1,0:T(8,128)S(1)} all-to-all(f32[8,6,8,128]{3,2,1,0:T(8,128)S(1)} %broadcast_in_dim.22), channel_id=1, replica_groups={{0,32,64,96,128,160,192,224},{16,48,80,112,144,176,208,240},{1,33,65,97..., dimensions={0} | all-to-all | bytes 393216 | tf_op jit(solution)/shard_map/all_to_all | solution.py:276
  64.5 0.1 spread.1
  64.5 15.1 %all_to_all.26.mine_ref = f32[16,12,8,128]{3,2,1,0:T(8,128)S(1)} all-to-all(f32[16,12,8,128]{3,2,1,0:T(8,128)S(1)} %spread.1), channel_id=1, replica_groups=mesh['row'=16,'col'=16] {'col'}, dimensions={0} | all-to-all | bytes 1572864 | tf_op jit(solution)/shard_map/all_to_all | solution.py:277
  79.6 3.6 %collective-permute-start = (f32[16,12,8,128]{3,2,1,0:T(8,128)S(1)}, f32[16,12,8,128]{3,2,1,0:T(8,128)S(1)}, u32[]{:S(2)}, u32[]{:S(2)}) collective-permute-start(f32[16,12,8,128]{3,2,1,0:T(8,128)S(1)} %all_to_all.26.mine_ref), channel_id=1, source_target_pairs={{0,16},{16,0},{32,48},{48,32},{64,80},{80,64},{96,112},{112,96},{1... | collective-permute-start | bytes 2359304 | tf_op jit(solution)/shard_map/ppermute | solution.py:278
  83.2 0.1 pad_add_fusion.place_ref
  83.3 1.4 %broadcast_in_dim.20 = f16[16,400,128]{2,1,0:T(8,128)(2,1)} broadcast(f16[400,128]{1,0:T(8,128)(2,1)S(1)} %concatenate.3), dimensions={1,2} | broadcast | bytes 1740800 | tf_op jit(solution)/shard_map/broadcast_in_dim | solution.py:280
  84.7 4.4 %all-to-all-start.3 = ((f16[16,400,128]{2,1,0:T(8,128)(2,1)}), f16[16,400,128]{2,1,0:T(8,128)(2,1)}, u32[]{:S(2)}, u32[]{:S(2)}) async-start(f16[16,400,128]{2,1,0:T(8,128)(2,1)} %broadcast_in_dim.20), calls=%async_computation.3 | async-start | bytes 3276800 | tf_op jit(solution)/shard_map/all_to_all | solution.py:281
  89.1 0.0 collective-permute-done.other_ref
  89.1 0.5 all-gather.2.cloned.1.call-done.top_hbm
  89.6 24.3 %chain.1 = (bf16[768,768]{1,0:T(8,128)(2,1)S(1)}, f32[6,128,128]{2,1,0:T(8,128)S(1)}, bf16[768,1024]{1,0:T(8,128)(2,1)}, f32[1,1]{1,0:T(1,128)}) custom-call(s32[2]{0:T(128)S(1)} %pad_add_fusion.place_ref, f32[16,12,8,128]{3,2,1,0:T(8,128)S(1)} %all_to_all.26.mine_ref, f32[16,12,8,128]{3,2,1,0:T(8,128)S(1)} %collective-permute-done.other_ref, ...), custom_call_target="tpu_custom_call" | custom-call | flops 30000001024 | bytes 4194304 | tf_op jit(solution)/shard_map/chain/pallas_call | solution.py:127
  113.9 0.0 copy-start
  113.9 2.8 %all-to-all-done.3 = f16[16,400,128]{2,1,0:T(8,128)(2,1)} async-done(((f16[16,400,128]{2,1,0:T(8,128)(2,1)}), f16[16,400,128]{2,1,0:T(8,128)(2,1)}, u32[]{:S(2)}, u32[]{:S(2)}) %all-to-all-start.3) | async-done | bytes 1638432 | tf_op jit(solution)/shard_map/all_to_all | solution.py:281
  116.8 1.6 %convert_element_type.15.rp_ref = f32[16,400,128]{2,1,0:T(8,128)S(1)} convert(f16[16,400,128]{2,1,0:T(8,128)(2,1)} %all-to-all-done.3) | non-fusion elementwise | flops 819200 | bytes 4915200 | tf_op jit(solution)/shard_map/convert_element_type | solution.py:284
  118.4 0.0 copy-done
  118.4 8.3 %finish.1 = (f32[8,6,128,128]{3,2,1,0:T(8,128)}, f32[8,8,128,128]{3,2,1,0:T(8,128)}) custom-call(s32[2]{0:T(128)S(1)} %pad_add_fusion.place_ref, f32[8,8,128,128]{3,2,1,0:T(8,128)} %bitcast.19, f32[16,400,128]{2,1,0:T(8,128)S(1)} %convert_element_type.15.rp_ref, bf16[768,1024]{1,0:T(8,128)(2,1)S(1)} %copy-done, ...), custom_call_target="tpu_custom_call" | custom-call | flops 4000000000 | bytes 14680064 | tf_op jit(solution)/shard_map/finish/pallas_call | solution.py:205
  (4 shorter events, 0.1 us)
Async XLA Ops:
  7.2 82.4 %all-gather.2.cloned.1.call-start = ((), (), s32[]{:S(2)}) async-start(), calls=%async_computation.4 | async-start | bytes 8912896 | tf_op jit(solution)/shard_map/all_gather | solution.py:272
  79.6 9.5 %collective-permute-start = (f32[16,12,8,128]{3,2,1,0:T(8,128)S(1)}, f32[16,12,8,128]{3,2,1,0:T(8,128)S(1)}, u32[]{:S(2)}, u32[]{:S(2)}) collective-permute-start(f32[16,12,8,128]{3,2,1,0:T(8,128)S(1)} %all_to_all.26.mine_ref), channel_id=1, source_target_pairs={{0,16},{16,0},{32,48},{48,32},{64,80},{80,64},{96,112},{112,96},{1... | collective-permute-start | bytes 2359304 | tf_op jit(solution)/shard_map/ppermute | solution.py:278
  84.7 32.1 %all-to-all-start.3 = ((f16[16,400,128]{2,1,0:T(8,128)(2,1)}), f16[16,400,128]{2,1,0:T(8,128)(2,1)}, u32[]{:S(2)}, u32[]{:S(2)}) async-start(f16[16,400,128]{2,1,0:T(8,128)(2,1)} %broadcast_in_dim.20), calls=%async_computation.3 | async-start | bytes 3276800 | tf_op jit(solution)/shard_map/all_to_all | solution.py:281
  113.9 4.5 %copy-start = (bf16[768,1024]{1,0:T(8,128)(2,1)S(1)}, bf16[768,1024]{1,0:T(8,128)(2,1)}, u32[]{:S(2)}) copy-start(bf16[768,1024]{1,0:T(8,128)(2,1)} %get-tuple-element.21.q_ref) | copy-start | bytes 4718596
Sparse Core Ops, SparseCore 0:
  25.2 64.3 all-gather.1

commit v5 on v3

--- a/solution.py
+++ b/solution.py
@@ -181,15 +181,20 @@
         store = pltpu.make_async_copy(p_ref.at[:, k], pf_hbm.at[:, k], p_sem.at[k])
         store.start()
         stores.append(store)
-    for n in range(pairs):
-        loads[n].wait()
-        upd = jnp.dot(b_ref[...], q_ref[:, 2 * n * NB:2 * (n + 1) * NB], preferred_element_type=jnp.float32)
-        for l in range(LT):
-            for m in range(2):
-                a_ref[n, l, m] = a_ref[n, l, m] - upd[l * NB:(l + 1) * NB, m * NB:(m + 1) * NB]
-        store = pltpu.make_async_copy(a_ref.at[n], tr_hbm.at[:, pl.ds(2 * n, 2)], t_sem.at[n])
-        store.start()
-        stores.append(store)
+        if k % 2 == 0:
+            continue
+        for n in range(pairs):
+            if k == 1:
+                loads[n].wait()
+            upd = jnp.dot(b_ref[:, (k - 1) * NB:(k + 1) * NB], q_ref[(k - 1) * NB:(k + 1) * NB, 2 * n * NB:2 * (n + 1) * NB],
+                          preferred_element_type=jnp.float32)
+            for l in range(LT):
+                for m in range(2):
+                    a_ref[n, l, m] = a_ref[n, l, m] - upd[l * NB:(l + 1) * NB, m * NB:(m + 1) * NB]
+            if k == STEPS - 1:
+                store = pltpu.make_async_copy(a_ref.at[n], tr_hbm.at[:, pl.ds(2 * n, 2)], t_sem.at[n])
+                store.start()
+                stores.append(store)
     for store in stores:
         store.wait()
 

time: 120 us -> 119 us (level)
  transfers between devices with their start and end apart: 3 -> 3, of which waited for: 2 -> 2; matrix products, arithmetic and copies ran while one was open for 3% -> 3% of each run, Pallas kernels for 20% -> 21%
where the time goes in v5:
time: 119 us; the launch traced here: 118 us
  blocking collectives  52.8 us (44%)
  Pallas kernels  32.6 us (27%)
  between operations  14.9 us (13%)
  starting transfers between devices  8.04 us (7%)
  local copies, waits for them, and re-layouts  4.39 us (4%)
  waiting for transfers between devices  3.35 us (3%)
  other arithmetic  2.36 us (2%)
    pallas_call x1, Pallas kernels, chain(): pl.pallas_call(chain_kernel, out_shape=(jax.ShapeDtypeStruct((STEPS * NB,...  24.3 us
    all_to_all x1, blocking collectives, shards(): lax.all_to_all(sent, 'row', 0, 0, tiled=True, axis_index_groups=groups)  19.8 us
    all_to_all x1, blocking collectives, shards(): lax.all_to_all(first, 'col', 0, 0, tiled=True).reshape(16, LT, 8, NB)  17.9 us
    all_to_all x1, blocking collectives, shards(): mine = lax.all_to_all(spread_half(lead), 'col', 0, 0, tiled=True)  15.1 us
    pallas_call x1, Pallas kernels, finish(): pl.pallas_call(finish_kernel, out_shape=(jax.ShapeDtypeStruct((LT, STEPS,...  8.27 us
    all_to_all x1, starting transfers between devices, shards(): down = lax.all_to_all(half, 'col', 0, 0, tiled=True)  4.4 us
    ppermute x1, starting transfers between devices, shards(): other = lax.ppermute(mine, 'row', [(i, i ^ 1) for i in range(16)])  3.6 us
    all_to_all x1, waiting for transfers between devices, shards(): down = lax.all_to_all(half, 'col', 0, 0, tiled=True)  2.57 us
  transfers between devices with their start and end apart: 3, of which 2 were waited for; matrix products, arithmetic and copies ran while one was open for 3% of the time, Pallas kernels for 21%

profile of v5, /device:TPU:1, one launch (start us, length us, event | category | flops | bytes accessed | tf_op | source)
XLA Modules:
  0.0 118.4 jit_solution(1394404458845162439)
XLA Ops:
  7.2 0.0 all-gather.3.cloned.1.call-start
  7.2 1.9 %slice.23 = f32[1,1,8,1,128,128]{5,4,3,2,1,0:T(8,128)} slice(f32[8,1,8,1,128,128]{5,4,3,2,1,0:T(8,128)} %param.1), slice={[0:1], [0:1], [0:8], [0:1], [0:128], [0:128]} | slice | bytes 1048576 | tf_op jit(solution)/shard_map/slice | solution.py:249
  9.1 0.0 all-gather.3.cloned.1.call-update
  9.1 1.1 copy_bitcast_fusion
  10.2 17.9 %all_to_all.24 = f32[16,64,128]{2,1,0:T(8,128)S(1)} all-to-all(f32[16,64,128]{2,1,0:T(8,128)S(1)} %copy_bitcast_fusion), channel_id=1, replica_groups=mesh['row'=16,'col'=16] {'col'}, dimensions={0} | all-to-all | bytes 1048576 | tf_op jit(solution)/shard_map/all_to_all | solution.py:251
  28.1 0.6 abs_reduce_fusion
  29.5 19.8 %all_to_all.25.x_ref = f32[8,6,8,128]{3,2,1,0:T(8,128)S(1)} all-to-all(f32[8,6,8,128]{3,2,1,0:T(8,128)S(1)} %broadcast_in_dim.22), channel_id=1, replica_groups={{0,32,64,96,128,160,192,224},{16,48,80,112,144,176,208,240},{1,33,65,97..., dimensions={0} | all-to-all | bytes 393216 | tf_op jit(solution)/shard_map/all_to_all | solution.py:254
  49.3 0.1 spread.1
  49.4 15.1 %all_to_all.26.mine_ref = f32[16,12,8,128]{3,2,1,0:T(8,128)S(1)} all-to-all(f32[16,12,8,128]{3,2,1,0:T(8,128)S(1)} %spread.1), channel_id=1, replica_groups=mesh['row'=16,'col'=16] {'col'}, dimensions={0} | all-to-all | bytes 1572864 | tf_op jit(solution)/shard_map/all_to_all | solution.py:255
  64.5 3.6 %collective-permute-start = (f32[16,12,8,128]{3,2,1,0:T(8,128)S(1)}, f32[16,12,8,128]{3,2,1,0:T(8,128)S(1)}, u32[]{:S(2)}, u32[]{:S(2)}) collective-permute-start(f32[16,12,8,128]{3,2,1,0:T(8,128)S(1)} %all_to_all.26.mine_ref), channel_id=1, source_target_pairs={{0,16},{16,0},{32,48},{48,32},{64,80},{80,64},{96,112},{112,96},{1... | collective-permute-start | bytes 2359304 | tf_op jit(solution)/shard_map/ppermute | solution.py:256
  68.1 0.1 pad_add_fusion.place_ref
  68.2 1.4 %broadcast_in_dim.20 = f16[16,400,128]{2,1,0:T(8,128)(2,1)} broadcast(f16[400,128]{1,0:T(8,128)(2,1)S(1)} %concatenate.3), dimensions={1,2} | broadcast | bytes 1740800 | tf_op jit(solution)/shard_map/broadcast_in_dim | solution.py:258
  69.6 4.4 %all-to-all-start.3 = ((f16[16,400,128]{2,1,0:T(8,128)(2,1)}), f16[16,400,128]{2,1,0:T(8,128)(2,1)}, u32[]{:S(2)}, u32[]{:S(2)}) async-start(f16[16,400,128]{2,1,0:T(8,128)(2,1)} %broadcast_in_dim.20), calls=%async_computation.3 | async-start | bytes 3276800 | tf_op jit(solution)/shard_map/all_to_all | solution.py:259
  74.0 0.0 collective-permute-done.other_ref
  74.0 0.8 all-gather.3.cloned.1.call-done
  74.8 24.3 %chain.1 = (bf16[768,768]{1,0:T(8,128)(2,1)S(1)}, f32[6,128,128]{2,1,0:T(8,128)S(1)}, bf16[768,1024]{1,0:T(8,128)(2,1)}, f32[1,1]{1,0:T(1,128)}) custom-call(s32[2]{0:T(128)S(1)} %pad_add_fusion.place_ref, f32[16,12,8,128]{3,2,1,0:T(8,128)S(1)} %all_to_all.26.mine_ref, f32[16,12,8,128]{3,2,1,0:T(8,128)S(1)} %collective-permute-done.other_ref, ...), custom_call_target="tpu_custom_call" | custom-call | flops 30000001024 | bytes 4194304 | tf_op jit(solution)/shard_map/chain/pallas_call | solution.py:127
  99.1 0.0 copy-start
  99.1 2.6 %all-to-all-done.3 = f16[16,400,128]{2,1,0:T(8,128)(2,1)} async-done(((f16[16,400,128]{2,1,0:T(8,128)(2,1)}), f16[16,400,128]{2,1,0:T(8,128)(2,1)}, u32[]{:S(2)}, u32[]{:S(2)}) %all-to-all-start.3) | async-done | bytes 1638432 | tf_op jit(solution)/shard_map/all_to_all | solution.py:259
  101.6 1.6 %convert_element_type.15.rp_ref = f32[16,400,128]{2,1,0:T(8,128)S(1)} convert(f16[16,400,128]{2,1,0:T(8,128)(2,1)} %all-to-all-done.3) | non-fusion elementwise | flops 819200 | bytes 4915200 | tf_op jit(solution)/shard_map/convert_element_type | solution.py:262
  103.3 0.0 copy-done
  103.3 8.3 %finish.1 = (f32[8,6,128,128]{3,2,1,0:T(8,128)}, f32[8,8,128,128]{3,2,1,0:T(8,128)}) custom-call(s32[2]{0:T(128)S(1)} %pad_add_fusion.place_ref, f32[8,8,128,128]{3,2,1,0:T(8,128)} %bitcast.25, f32[16,400,128]{2,1,0:T(8,128)S(1)} %convert_element_type.15.rp_ref, bf16[768,1024]{1,0:T(8,128)(2,1)S(1)} %copy-done, ...), custom_call_target="tpu_custom_call" | custom-call | flops 4000000000 | bytes 14680064 | tf_op jit(solution)/shard_map/finish/pallas_call | solution.py:205
  (4 shorter events, 0.1 us)
Async XLA Ops:
  7.2 67.6 %all-gather.3.cloned.1.call-start = ((), (), s32[]{:S(2)}) async-start(), calls=%async_computation.4 | async-start | bytes 8912896 | tf_op jit(solution)/shard_map/all_gather | solution.py:249
  64.5 9.5 %collective-permute-start = (f32[16,12,8,128]{3,2,1,0:T(8,128)S(1)}, f32[16,12,8,128]{3,2,1,0:T(8,128)S(1)}, u32[]{:S(2)}, u32[]{:S(2)}) collective-permute-start(f32[16,12,8,128]{3,2,1,0:T(8,128)S(1)} %all_to_all.26.mine_ref), channel_id=1, source_target_pairs={{0,16},{16,0},{32,48},{48,32},{64,80},{80,64},{96,112},{112,96},{1... | collective-permute-start | bytes 2359304 | tf_op jit(solution)/shard_map/ppermute | solution.py:256
  69.6 32.0 %all-to-all-start.3 = ((f16[16,400,128]{2,1,0:T(8,128)(2,1)}), f16[16,400,128]{2,1,0:T(8,128)(2,1)}, u32[]{:S(2)}, u32[]{:S(2)}) async-start(f16[16,400,128]{2,1,0:T(8,128)(2,1)} %broadcast_in_dim.20), calls=%async_computation.3 | async-start | bytes 3276800 | tf_op jit(solution)/shard_map/all_to_all | solution.py:259
  99.1 4.2 %copy-start = (bf16[768,1024]{1,0:T(8,128)(2,1)S(1)}, bf16[768,1024]{1,0:T(8,128)(2,1)}, u32[]{:S(2)}) copy-start(bf16[768,1024]{1,0:T(8,128)(2,1)} %get-tuple-element.17.q_ref) | copy-start | bytes 4718596
Sparse Core Ops, SparseCore 0:
  10.4 64.3 all-gather.2

commit v6 on v5

--- a/solution.py
+++ b/solution.py
@@ -250,12 +250,14 @@
     first = matrix[:, 0].reshape(LT, 16, 8, NB).transpose(1, 0, 2, 3).reshape(16 * LT * 8, NB)
     slabs = lax.all_to_all(first, "col", 0, 0, tiled=True).reshape(16, LT, 8, NB)[:STEPS]
     sent = jnp.broadcast_to(slabs[None, :, 0], (8, STEPS, 8, NB))
+    sent, slabs = lax.optimization_barrier((sent, slabs))
     groups = [[2 * z + c for z in range(8)] for c in range(2)]
     lead = lax.all_to_all(sent, "row", 0, 0, tiled=True, axis_index_groups=groups)
-    mine = lax.all_to_all(spread_half(lead), "col", 0, 0, tiled=True)
+    half = packed(slabs.reshape(STEPS * LT * 8, NB))
+    half, lead = lax.optimization_barrier((jnp.broadcast_to(half[None], (16,) + half.shape), spread_half(lead)))
+    mine = lax.all_to_all(lead, "col", 0, 0, tiled=True)
+    half, mine = lax.optimization_barrier((half, mine))
     other = lax.ppermute(mine, "row", [(i, i ^ 1) for i in range(16)])
-    half = packed(slabs.reshape(STEPS * LT * 8, NB))
-    half, mine = lax.optimization_barrier((jnp.broadcast_to(half[None], (16,) + half.shape), mine))
     down = lax.all_to_all(half, "col", 0, 0, tiled=True)
     ub, linv, q, logdet = chain(place, mine, other, across)
     down, q = lax.optimization_barrier((down, q))

time: 119 us -> 118 us (level)
  blocking collectives: 52.8 us -> 32.9 us
  waiting for transfers between devices: 3.35 us -> 13.8 us
  starting transfers between devices: 8.04 us -> 16.2 us
    all_to_all x2 -> x1, blocking collectives: 34.9 us -> 15.1 us  [shards(): mine = lax.all_to_all(lead, 'col', 0, 0, tiled=True)]
    all_to_all x0 -> x1, waiting for transfers between devices: none -> 10.4 us  [shards(): lax.all_to_all(sent, 'row', 0, 0, tiled=True, axis_index_groups=groups)]
    all_to_all x0 -> x1, starting transfers between devices: none -> 8.19 us  [shards(): lax.all_to_all(sent, 'row', 0, 0, tiled=True, axis_index_groups=groups)]
  transfers between devices with their start and end apart: 3 -> 4, of which waited for: 2 -> 3; matrix products, arithmetic and copies ran while one was open for 3% -> 3% of each run, Pallas kernels for 21% -> 21%
where the time goes in v6:
time: 118 us
  blocking collectives  32.9 us (28%)
  Pallas kernels  32.6 us (28%)
  starting transfers between devices  16.2 us (14%)
  between operations  14.9 us (13%)
  waiting for transfers between devices  13.8 us (12%)
  local copies, waits for them, and re-layouts  5.09 us (4%)
  other arithmetic  2.35 us (2%)
    pallas_call x1, Pallas kernels, chain(): pl.pallas_call(chain_kernel, out_shape=(jax.ShapeDtypeStruct((STEPS * NB,...  24.3 us
    all_to_all x1, blocking collectives, shards(): lax.all_to_all(first, 'col', 0, 0, tiled=True).reshape(16, LT, 8, NB)  17.9 us
    all_to_all x1, blocking collectives, shards(): mine = lax.all_to_all(lead, 'col', 0, 0, tiled=True)  15.1 us
    all_to_all x1, waiting for transfers between devices, shards(): lax.all_to_all(sent, 'row', 0, 0, tiled=True, axis_index_groups=groups)  10.4 us
    pallas_call x1, Pallas kernels, finish(): pl.pallas_call(finish_kernel, out_shape=(jax.ShapeDtypeStruct((LT, STEPS,...  8.27 us
    all_to_all x1, starting transfers between devices, shards(): lax.all_to_all(sent, 'row', 0, 0, tiled=True, axis_index_groups=groups)  8.19 us
    all_to_all x1, starting transfers between devices, shards(): down = lax.all_to_all(half, 'col', 0, 0, tiled=True)  4.4 us
    ppermute x1, starting transfers between devices, shards(): other = lax.ppermute(mine, 'row', [(i, i ^ 1) for i in range(16)])  3.62 us
  transfers between devices with their start and end apart: 4, of which 3 were waited for; matrix products, arithmetic and copies ran while one was open for 3% of the time, Pallas kernels for 21%

profile of v6, /device:TPU:1, one launch (start us, length us, event | category | flops | bytes accessed | tf_op | source)
XLA Modules:
  0.0 117.9 jit_solution(7822600414289755750)
XLA Ops:
  7.2 0.0 all-gather.3.cloned.1.call-start
  7.2 1.9 %slice.23 = f32[1,1,8,1,128,128]{5,4,3,2,1,0:T(8,128)} slice(f32[8,1,8,1,128,128]{5,4,3,2,1,0:T(8,128)} %param.1), slice={[0:1], [0:1], [0:8], [0:1], [0:128], [0:128]} | slice | bytes 1048576 | tf_op jit(solution)/shard_map/slice | solution.py:249
  9.1 0.0 all-gather.3.cloned.1.call-update
  9.1 1.1 copy_bitcast_fusion
  10.2 17.9 %all_to_all.24 = f32[16,64,128]{2,1,0:T(8,128)S(1)} all-to-all(f32[16,64,128]{2,1,0:T(8,128)S(1)} %copy_bitcast_fusion), channel_id=1, replica_groups=mesh['row'=16,'col'=16] {'col'}, dimensions={0} | all-to-all | bytes 1048576 | tf_op jit(solution)/shard_map/all_to_all | solution.py:251
  28.1 0.7 broadcast_in_dim.21
  28.8 8.2 %all-to-all-start.1 = ((f32[8,6,8,128]{3,2,1,0:T(8,128)}), f32[8,6,8,128]{3,2,1,0:T(8,128)S(1)}, u32[]{:S(2)}, u32[]{:S(2)}) async-start(f32[8,6,8,128]{3,2,1,0:T(8,128)} %broadcast_in_dim.21), calls=%async_computation.1 | async-start | bytes 393216 | tf_op jit(solution)/shard_map/all_to_all | solution.py:255
  37.0 0.6 abs_reduce_fusion
  38.4 10.4 %all-to-all-done.1.x_ref = f32[8,6,8,128]{3,2,1,0:T(8,128)S(1)} async-done(((f32[8,6,8,128]{3,2,1,0:T(8,128)}), f32[8,6,8,128]{3,2,1,0:T(8,128)S(1)}, u32[]{:S(2)}, u32[]{:S(2)}) %all-to-all-start.1) | async-done | bytes 196640 | tf_op jit(solution)/shard_map/all_to_all | solution.py:255
  48.9 0.1 spread.1
  48.9 1.4 %broadcast_in_dim.22 = f16[16,400,128]{2,1,0:T(8,128)(2,1)} broadcast(f16[400,128]{1,0:T(8,128)(2,1)S(1)} %concatenate.3), dimensions={1,2} | broadcast | bytes 1740800 | tf_op jit(solution)/shard_map/broadcast_in_dim | solution.py:257
  50.3 15.1 %all_to_all.25.mine_ref = f32[16,12,8,128]{3,2,1,0:T(8,128)S(1)} all-to-all(f32[16,12,8,128]{3,2,1,0:T(8,128)S(1)} %spread.1), channel_id=1, replica_groups=mesh['row'=16,'col'=16] {'col'}, dimensions={0} | all-to-all | bytes 1572864 | tf_op jit(solution)/shard_map/all_to_all | solution.py:258
  65.4 3.6 %collective-permute-start = (f32[16,12,8,128]{3,2,1,0:T(8,128)S(1)}, f32[16,12,8,128]{3,2,1,0:T(8,128)S(1)}, u32[]{:S(2)}, u32[]{:S(2)}) collective-permute-start(f32[16,12,8,128]{3,2,1,0:T(8,128)S(1)} %all_to_all.25.mine_ref), channel_id=1, source_target_pairs={{0,16},{16,0},{32,48},{48,32},{64,80},{80,64},{96,112},{112,96},{1... | collective-permute-start | bytes 2359304 | tf_op jit(solution)/shard_map/ppermute | solution.py:260
  69.0 0.1 pad_add_fusion.place_ref
  69.1 4.4 %all-to-all-start.3 = ((f16[16,400,128]{2,1,0:T(8,128)(2,1)}), f16[16,400,128]{2,1,0:T(8,128)(2,1)}, u32[]{:S(2)}, u32[]{:S(2)}) async-start(f16[16,400,128]{2,1,0:T(8,128)(2,1)} %broadcast_in_dim.22), calls=%async_computation.3 | async-start | bytes 3276800 | tf_op jit(solution)/shard_map/all_to_all | solution.py:261
  73.5 0.0 collective-permute-done.other_ref
  73.5 1.3 %all-gather.3.cloned.1.call-done = f32[16,1,8,1,128,128]{5,4,3,2,1,0:T(8,128)} async-done(((f32[1,1,8,1,128,128]{5,4,3,2,1,0:T(8,128)}), f32[16,1,8,1,128,128]{5,4,3,2,1,0:T(8,128)}) %all-gather.3.cloned.1.call-update) | async-done | bytes 8388624 | tf_op jit(solution)/shard_map/all_gather | solution.py:249
  74.8 24.3 %chain.1 = (bf16[768,768]{1,0:T(8,128)(2,1)S(1)}, f32[6,128,128]{2,1,0:T(8,128)S(1)}, bf16[768,1024]{1,0:T(8,128)(2,1)}, f32[1,1]{1,0:T(1,128)}) custom-call(s32[2]{0:T(128)S(1)} %pad_add_fusion.place_ref, f32[16,12,8,128]{3,2,1,0:T(8,128)S(1)} %all_to_all.25.mine_ref, f32[16,12,8,128]{3,2,1,0:T(8,128)S(1)} %collective-permute-done.other_ref, ...), custom_call_target="tpu_custom_call" | custom-call | flops 30000001024 | bytes 4194304 | tf_op jit(solution)/shard_map/chain/pallas_call | solution.py:127
  99.1 0.0 copy-start
  99.1 2.0 %all-to-all-done.3 = f16[16,400,128]{2,1,0:T(8,128)(2,1)} async-done(((f16[16,400,128]{2,1,0:T(8,128)(2,1)}), f16[16,400,128]{2,1,0:T(8,128)(2,1)}, u32[]{:S(2)}, u32[]{:S(2)}) %all-to-all-start.3) | async-done | bytes 1638432 | tf_op jit(solution)/shard_map/all_to_all | solution.py:261
  101.1 1.6 %convert_element_type.15.rp_ref = f32[16,400,128]{2,1,0:T(8,128)S(1)} convert(f16[16,400,128]{2,1,0:T(8,128)(2,1)} %all-to-all-done.3) | non-fusion elementwise | flops 819200 | bytes 4915200 | tf_op jit(solution)/shard_map/convert_element_type | solution.py:264
  102.8 0.0 copy-done
  102.8 8.3 %finish.1 = (f32[8,6,128,128]{3,2,1,0:T(8,128)}, f32[8,8,128,128]{3,2,1,0:T(8,128)}) custom-call(s32[2]{0:T(128)S(1)} %pad_add_fusion.place_ref, f32[8,8,128,128]{3,2,1,0:T(8,128)} %bitcast.25, f32[16,400,128]{2,1,0:T(8,128)S(1)} %convert_element_type.15.rp_ref, bf16[768,1024]{1,0:T(8,128)(2,1)S(1)} %copy-done, ...), custom_call_target="tpu_custom_call" | custom-call | flops 4000000000 | bytes 14680064 | tf_op jit(solution)/shard_map/finish/pallas_call | solution.py:205
  (4 shorter events, 0.1 us)
Async XLA Ops:
  7.2 67.6 %all-gather.3.cloned.1.call-start = ((), (), s32[]{:S(2)}) async-start(), calls=%async_computation.4 | async-start | bytes 8912896 | tf_op jit(solution)/shard_map/all_gather | solution.py:249
  28.8 20.0 %all-to-all-start.1 = ((f32[8,6,8,128]{3,2,1,0:T(8,128)}), f32[8,6,8,128]{3,2,1,0:T(8,128)S(1)}, u32[]{:S(2)}, u32[]{:S(2)}) async-start(f32[8,6,8,128]{3,2,1,0:T(8,128)} %broadcast_in_dim.21), calls=%async_computation.1 | async-start | bytes 393216 | tf_op jit(solution)/shard_map/all_to_all | solution.py:255
  65.4 8.1 %collective-permute-start = (f32[16,12,8,128]{3,2,1,0:T(8,128)S(1)}, f32[16,12,8,128]{3,2,1,0:T(8,128)S(1)}, u32[]{:S(2)}, u32[]{:S(2)}) collective-permute-start(f32[16,12,8,128]{3,2,1,0:T(8,128)S(1)} %all_to_all.25.mine_ref), channel_id=1, source_target_pairs={{0,16},{16,0},{32,48},{48,32},{64,80},{80,64},{96,112},{112,96},{1... | collective-permute-start | bytes 2359304 | tf_op jit(solution)/shard_map/ppermute | solution.py:260
  69.1 32.1 %all-to-all-start.3 = ((f16[16,400,128]{2,1,0:T(8,128)(2,1)}), f16[16,400,128]{2,1,0:T(8,128)(2,1)}, u32[]{:S(2)}, u32[]{:S(2)}) async-start(f16[16,400,128]{2,1,0:T(8,128)(2,1)} %broadcast_in_dim.22), calls=%async_computation.3 | async-start | bytes 3276800 | tf_op jit(solution)/shard_map/all_to_all | solution.py:261
  99.1 3.7 %copy-start = (bf16[768,1024]{1,0:T(8,128)(2,1)S(1)}, bf16[768,1024]{1,0:T(8,128)(2,1)}, u32[]{:S(2)}) copy-start(bf16[768,1024]{1,0:T(8,128)(2,1)} %get-tuple-element.25.q_ref) | copy-start | bytes 4718596
Sparse Core Ops, SparseCore 0:
  10.4 64.3 all-gather.2

commit v7 on v6

--- a/solution.py
+++ b/solution.py
@@ -66,22 +66,47 @@
             nb = SB // 8
             R = [[w_ref[r0 + 8 * b:r0 + 8 * b + 8, t * NB:(t + 1) * NB] for b in range(nb)] for t in wide]
             cols = [{b: jnp.broadcast_to(R[0][b][:, r0 + q:r0 + q + 1], (8, NB)) for b in range(q // 8, nb)} for q in range(SB)]
-            for p in range(SB):
+            for p in range(0, SB, 4):
                 pb, pr = p // 8, p % 8
-                inv = lax.rsqrt(jnp.broadcast_to(cols[p][pb][pr:pr + 1, :], (8, NB)))
-                l = {b: cols[p][b] * inv for b in range(pb, nb)}
-                for q in range(p + 1, SB):
-                    m = jnp.broadcast_to(l[q // 8][q % 8:q % 8 + 1, :], (8, NB))
-                    for b in range(q // 8, nb):
-                        cols[q][b] = cols[q][b] - l[b] * m
+                c = [[None] * 4 for _ in range(4)]
+                for i in range(4):
+                    for j in range(i + 1):
+                        c[i][j] = jnp.broadcast_to(cols[p + j][pb][pr + i:pr + i + 1, :], (8, NB))
+                inv = [None] * 4
+                l = [None] * 4
+                for j in range(4):
+                    inv[j] = lax.rsqrt(c[j][j])
+                    for i in range(j + 1, 4):
+                        c[i][j] = c[i][j] * inv[j]
+                    for i in range(j + 1, 4):
+                        for m in range(j + 1, i + 1):
+                            c[i][m] = c[i][m] - c[i][j] * c[m][j]
+                    x = {b: cols[p + j][b] for b in range(pb, nb)}
+                    for m in range(j):
+                        x = {b: x[b] - l[m][b] * c[j][m] for b in x}
+                    l[j] = {b: x[b] * inv[j] for b in x}
+                for q in range(p + 4, SB):
+                    for j in range(4):
+                        m = jnp.broadcast_to(l[j][q // 8][q % 8:q % 8 + 1, :], (8, NB))
+                        for b in range(q // 8, nb):
+                            cols[q][b] = cols[q][b] - l[j][b] * m
                 for t in range(2):
-                    u = jnp.broadcast_to(R[t][pb][pr:pr + 1, :], (8, NB)) * inv
-                    if pr < 7:
-                        R[t][pb] = jnp.where(rows8 == pr, u, R[t][pb] - jnp.where(rows8 > pr, l[pb], 0.0) * u)
-                    else:
-                        R[t][pb] = jnp.where(rows8 == pr, u, R[t][pb])
+                    u = []
+                    for j in range(4):
+                        x = jnp.broadcast_to(R[t][pb][pr + j:pr + j + 1, :], (8, NB))
+                        for m in range(j):
+                            x = x - c[j][m] * u[m]
+                        u.append(x * inv[j])
+                    own = R[t][pb]
+                    if pr + 4 < 8:
+                        for j in range(4):
+                            own = own - jnp.where(rows8 >= pr + 4, l[j][pb], 0.0) * u[j]
+                    for j in range(4):
+                        own = jnp.where(rows8 == pr + j, u[j], own)
+                    R[t][pb] = own
                     for b in range(pb + 1, nb):
-                        R[t][b] = R[t][b] - l[b] * u
+                        for j in range(4):
+                            R[t][b] = R[t][b] - l[j][b] * u[j]
             R = [jnp.concatenate(x, axis=0) for x in R]
             for t in range(2):
                 w_ref[r0:r0 + SB, wide[t] * NB:(wide[t] + 1) * NB] = R[t]
@@ -239,7 +264,7 @@
     top = jnp.maximum(jnp.max(jnp.abs(x)), 1e-30)
     power = jnp.floor(jnp.log2(top))
     body = (x * jnp.exp2(SHIFT - power)).astype(jnp.float16)
-    return jnp.concatenate([body, jnp.full((16, NB), power, jnp.float16)], axis=0)
+    return jnp.concatenate([body, jnp.full((8, NB), power, jnp.float16)], axis=0)
 
 
 def shards(covariance):

time: 118 us -> 118 us (level)
  no operation moved by 1% of the time
where the time goes in v7:
time: 118 us; the launch traced here: 117 us
  blocking collectives  32.9 us (28%)
  Pallas kernels  32.9 us (28%)
  starting transfers between devices  16.2 us (14%)
  between operations  14.9 us (13%)
  waiting for transfers between devices  13.1 us (11%)
  local copies, waits for them, and re-layouts  5.07 us (4%)
  other arithmetic  2.34 us (2%)
    pallas_call x1, Pallas kernels, chain(): pl.pallas_call(chain_kernel, out_shape=(jax.ShapeDtypeStruct((STEPS * NB,...  24.5 us
    all_to_all x1, blocking collectives, shards(): lax.all_to_all(first, 'col', 0, 0, tiled=True).reshape(16, LT, 8, NB)  17.9 us
    all_to_all x1, blocking collectives, shards(): mine = lax.all_to_all(lead, 'col', 0, 0, tiled=True)  15.1 us
    all_to_all x1, waiting for transfers between devices, shards(): lax.all_to_all(sent, 'row', 0, 0, tiled=True, axis_index_groups=groups)  10.4 us
    pallas_call x1, Pallas kernels, finish(): pl.pallas_call(finish_kernel, out_shape=(jax.ShapeDtypeStruct((LT, STEPS,...  8.27 us
    all_to_all x1, starting transfers between devices, shards(): lax.all_to_all(sent, 'row', 0, 0, tiled=True, axis_index_groups=groups)  8.19 us
    all_to_all x1, starting transfers between devices, shards(): down = lax.all_to_all(half, 'col', 0, 0, tiled=True)  4.4 us
    ppermute x1, starting transfers between devices, shards(): other = lax.ppermute(mine, 'row', [(i, i ^ 1) for i in range(16)])  3.62 us
  transfers between devices with their start and end apart: 4, of which 3 were waited for; matrix products, arithmetic and copies ran while one was open for 3% of the time, Pallas kernels for 21%

profile of v7, /device:TPU:1, one launch (start us, length us, event | category | flops | bytes accessed | tf_op | source)
XLA Modules:
  0.0 117.4 jit_solution(7419937108570988024)
XLA Ops:
  7.2 0.0 all-gather.3.cloned.1.call-start
  7.2 1.9 %slice.23 = f32[1,1,8,1,128,128]{5,4,3,2,1,0:T(8,128)} slice(f32[8,1,8,1,128,128]{5,4,3,2,1,0:T(8,128)} %param.1), slice={[0:1], [0:1], [0:8], [0:1], [0:128], [0:128]} | slice | bytes 1048576 | tf_op jit(solution)/shard_map/slice | solution.py:274
  9.1 0.0 all-gather.3.cloned.1.call-update
  9.1 1.1 copy_bitcast_fusion
  10.2 17.9 %all_to_all.24 = f32[16,64,128]{2,1,0:T(8,128)S(1)} all-to-all(f32[16,64,128]{2,1,0:T(8,128)S(1)} %copy_bitcast_fusion), channel_id=1, replica_groups=mesh['row'=16,'col'=16] {'col'}, dimensions={0} | all-to-all | bytes 1048576 | tf_op jit(solution)/shard_map/all_to_all | solution.py:276
  28.1 0.7 broadcast_in_dim.21
  28.8 8.2 %all-to-all-start.1 = ((f32[8,6,8,128]{3,2,1,0:T(8,128)}), f32[8,6,8,128]{3,2,1,0:T(8,128)S(1)}, u32[]{:S(2)}, u32[]{:S(2)}) async-start(f32[8,6,8,128]{3,2,1,0:T(8,128)} %broadcast_in_dim.21), calls=%async_computation.1 | async-start | bytes 393216 | tf_op jit(solution)/shard_map/all_to_all | solution.py:280
  37.0 0.6 abs_reduce_fusion
  38.4 10.4 %all-to-all-done.1.x_ref = f32[8,6,8,128]{3,2,1,0:T(8,128)S(1)} async-done(((f32[8,6,8,128]{3,2,1,0:T(8,128)}), f32[8,6,8,128]{3,2,1,0:T(8,128)S(1)}, u32[]{:S(2)}, u32[]{:S(2)}) %all-to-all-start.1) | async-done | bytes 196640 | tf_op jit(solution)/shard_map/all_to_all | solution.py:280
  48.9 0.1 spread.1
  48.9 1.4 %broadcast_in_dim.22 = f16[16,392,128]{2,1,0:T(8,128)(2,1)} broadcast(f16[392,128]{1,0:T(8,128)(2,1)S(1)} %concatenate.3), dimensions={1,2} | broadcast | bytes 1705984 | tf_op jit(solution)/shard_map/broadcast_in_dim | solution.py:282
  50.3 15.1 %all_to_all.25.mine_ref = f32[16,12,8,128]{3,2,1,0:T(8,128)S(1)} all-to-all(f32[16,12,8,128]{3,2,1,0:T(8,128)S(1)} %spread.1), channel_id=1, replica_groups=mesh['row'=16,'col'=16] {'col'}, dimensions={0} | all-to-all | bytes 1572864 | tf_op jit(solution)/shard_map/all_to_all | solution.py:283
  65.3 3.6 %collective-permute-start = (f32[16,12,8,128]{3,2,1,0:T(8,128)S(1)}, f32[16,12,8,128]{3,2,1,0:T(8,128)S(1)}, u32[]{:S(2)}, u32[]{:S(2)}) collective-permute-start(f32[16,12,8,128]{3,2,1,0:T(8,128)S(1)} %all_to_all.25.mine_ref), channel_id=1, source_target_pairs={{0,16},{16,0},{32,48},{48,32},{64,80},{80,64},{96,112},{112,96},{1... | collective-permute-start | bytes 2359304 | tf_op jit(solution)/shard_map/ppermute | solution.py:285
  69.0 0.1 pad_add_fusion.place_ref
  69.0 4.4 %all-to-all-start.3 = ((f16[16,392,128]{2,1,0:T(8,128)(2,1)}), f16[16,392,128]{2,1,0:T(8,128)(2,1)}, u32[]{:S(2)}, u32[]{:S(2)}) async-start(f16[16,392,128]{2,1,0:T(8,128)(2,1)} %broadcast_in_dim.22), calls=%async_computation.3 | async-start | bytes 3211264 | tf_op jit(solution)/shard_map/all_to_all | solution.py:286
  73.5 0.0 collective-permute-done.other_ref
  73.5 1.3 %all-gather.3.cloned.1.call-done = f32[16,1,8,1,128,128]{5,4,3,2,1,0:T(8,128)} async-done(((f32[1,1,8,1,128,128]{5,4,3,2,1,0:T(8,128)}), f32[16,1,8,1,128,128]{5,4,3,2,1,0:T(8,128)}) %all-gather.3.cloned.1.call-update) | async-done | bytes 8388624 | tf_op jit(solution)/shard_map/all_gather | solution.py:274
  74.8 24.5 %chain.1 = (bf16[768,768]{1,0:T(8,128)(2,1)S(1)}, f32[6,128,128]{2,1,0:T(8,128)S(1)}, bf16[768,1024]{1,0:T(8,128)(2,1)}, f32[1,1]{1,0:T(1,128)}) custom-call(s32[2]{0:T(128)S(1)} %pad_add_fusion.place_ref, f32[16,12,8,128]{3,2,1,0:T(8,128)S(1)} %all_to_all.25.mine_ref, f32[16,12,8,128]{3,2,1,0:T(8,128)S(1)} %collective-permute-done.other_ref, ...), custom_call_target="tpu_custom_call" | custom-call | flops 30000001024 | bytes 4194304 | tf_op jit(solution)/shard_map/chain/pallas_call | solution.py:152
  99.3 0.0 copy-start
  99.3 1.3 %all-to-all-done.3 = f16[16,392,128]{2,1,0:T(8,128)(2,1)} async-done(((f16[16,392,128]{2,1,0:T(8,128)(2,1)}), f16[16,392,128]{2,1,0:T(8,128)(2,1)}, u32[]{:S(2)}, u32[]{:S(2)}) %all-to-all-start.3) | async-done | bytes 1605664 | tf_op jit(solution)/shard_map/all_to_all | solution.py:286
  100.7 1.6 %convert_element_type.15.rp_ref = f32[16,392,128]{2,1,0:T(8,128)S(1)} convert(f16[16,392,128]{2,1,0:T(8,128)(2,1)} %all-to-all-done.3) | non-fusion elementwise | flops 802816 | bytes 4816896 | tf_op jit(solution)/shard_map/convert_element_type | solution.py:289
  102.3 0.0 copy-done
  102.3 8.3 %finish.1 = (f32[8,6,128,128]{3,2,1,0:T(8,128)}, f32[8,8,128,128]{3,2,1,0:T(8,128)}) custom-call(s32[2]{0:T(128)S(1)} %pad_add_fusion.place_ref, f32[8,8,128,128]{3,2,1,0:T(8,128)} %bitcast.25, f32[16,392,128]{2,1,0:T(8,128)S(1)} %convert_element_type.15.rp_ref, bf16[768,1024]{1,0:T(8,128)(2,1)S(1)} %copy-done, ...), custom_call_target="tpu_custom_call" | custom-call | flops 4000000000 | bytes 14680064 | tf_op jit(solution)/shard_map/finish/pallas_call | solution.py:230
  (4 shorter events, 0.1 us)
Async XLA Ops:
  7.2 67.6 %all-gather.3.cloned.1.call-start = ((), (), s32[]{:S(2)}) async-start(), calls=%async_computation.4 | async-start | bytes 8912896 | tf_op jit(solution)/shard_map/all_gather | solution.py:274
  28.8 20.0 %all-to-all-start.1 = ((f32[8,6,8,128]{3,2,1,0:T(8,128)}), f32[8,6,8,128]{3,2,1,0:T(8,128)S(1)}, u32[]{:S(2)}, u32[]{:S(2)}) async-start(f32[8,6,8,128]{3,2,1,0:T(8,128)} %broadcast_in_dim.21), calls=%async_computation.1 | async-start | bytes 393216 | tf_op jit(solution)/shard_map/all_to_all | solution.py:280
  65.3 8.1 %collective-permute-start = (f32[16,12,8,128]{3,2,1,0:T(8,128)S(1)}, f32[16,12,8,128]{3,2,1,0:T(8,128)S(1)}, u32[]{:S(2)}, u32[]{:S(2)}) collective-permute-start(f32[16,12,8,128]{3,2,1,0:T(8,128)S(1)} %all_to_all.25.mine_ref), channel_id=1, source_target_pairs={{0,16},{16,0},{32,48},{48,32},{64,80},{80,64},{96,112},{112,96},{1... | collective-permute-start | bytes 2359304 | tf_op jit(solution)/shard_map/ppermute | solution.py:285
  69.0 31.6 %all-to-all-start.3 = ((f16[16,392,128]{2,1,0:T(8,128)(2,1)}), f16[16,392,128]{2,1,0:T(8,128)(2,1)}, u32[]{:S(2)}, u32[]{:S(2)}) async-start(f16[16,392,128]{2,1,0:T(8,128)(2,1)} %broadcast_in_dim.22), calls=%async_computation.3 | async-start | bytes 3211264 | tf_op jit(solution)/shard_map/all_to_all | solution.py:286
  99.3 3.0 %copy-start = (bf16[768,1024]{1,0:T(8,128)(2,1)S(1)}, bf16[768,1024]{1,0:T(8,128)(2,1)}, u32[]{:S(2)}) copy-start(bf16[768,1024]{1,0:T(8,128)(2,1)} %get-tuple-element.25.q_ref) | copy-start | bytes 4718596
Sparse Core Ops, SparseCore 0:
  10.4 64.3 all-gather.2

commit v8 on v6

--- a/solution.py
+++ b/solution.py
@@ -134,18 +134,15 @@
         out_specs=(pl.BlockSpec(memory_space=pltpu.VMEM),) * 4,
         scratch_shapes=[pltpu.VMEM((NB, (STEPS + 1) * NB), jnp.float32), pltpu.VMEM((2, HALF, NB, NB), jnp.float32),
                         pltpu.VMEM((STEPS, LT, NB, NB), jnp.float32), pltpu.SemaphoreType.DMA],
-        compiler_params=pltpu.CompilerParams(vmem_limit_bytes=50 * 2**20),
+        compiler_params=pltpu.CompilerParams(vmem_limit_bytes=47 * 2**20),
         cost_estimate=pl.CostEstimate(flops=30_000_000_000, bytes_accessed=4 * 2**20, transcendentals=0),
         name="chain",
     )(place, mine, other, top)
 
 
-def finish_kernel(place_ref, a_hbm, rp_ref, q_ref, ub_ref, linv_ref, pf_hbm, tr_hbm, a_ref, p_ref, b_ref, in_sem, p_sem, t_sem):
+def finish_kernel(place_ref, a_ref, rp_ref, q_ref, ub_ref, linv_ref, pf_hbm, tr_hbm, t_ref, p_ref, b_ref, p_sem, t_sem):
     row = place_ref[0]
     pairs = LT // 2
-    loads = [pltpu.make_async_copy(a_hbm.at[:, pl.ds(2 * n, 2)], a_ref.at[n], in_sem.at[n]) for n in range(pairs)]
-    for copy in loads:
-        copy.start()
     ri = lax.broadcasted_iota(jnp.int32, (NB, NB), 0)
     ci = lax.broadcasted_iota(jnp.int32, (NB, NB), 1)
     scale = jnp.exp2(rp_ref[:, STEPS * LT * 8:STEPS * LT * 8 + 8] - SHIFT).reshape(NB, NB)
@@ -184,15 +181,14 @@
         if k % 2 == 0:
             continue
         for n in range(pairs):
-            if k == 1:
-                loads[n].wait()
             upd = jnp.dot(b_ref[:, (k - 1) * NB:(k + 1) * NB], q_ref[(k - 1) * NB:(k + 1) * NB, 2 * n * NB:2 * (n + 1) * NB],
                           preferred_element_type=jnp.float32)
             for l in range(LT):
                 for m in range(2):
-                    a_ref[n, l, m] = a_ref[n, l, m] - upd[l * NB:(l + 1) * NB, m * NB:(m + 1) * NB]
+                    before = a_ref[l, 2 * n + m] if k == 1 else t_ref[n, l, m]
+                    t_ref[n, l, m] = before - upd[l * NB:(l + 1) * NB, m * NB:(m + 1) * NB]
             if k == STEPS - 1:
-                store = pltpu.make_async_copy(a_ref.at[n], tr_hbm.at[:, pl.ds(2 * n, 2)], t_sem.at[n])
+                store = pltpu.make_async_copy(t_ref.at[n], tr_hbm.at[:, pl.ds(2 * n, 2)], t_sem.at[n])
                 store.start()
                 stores.append(store)
     for store in stores:
@@ -206,12 +202,12 @@
         finish_kernel,
         out_shape=(jax.ShapeDtypeStruct((LT, STEPS, NB, NB), jnp.float32),
                    jax.ShapeDtypeStruct((LT, LT, NB, NB), jnp.float32)),
-        in_specs=[pl.BlockSpec(memory_space=pltpu.SMEM), hb, vm, vm, vm, vm],
+        in_specs=[pl.BlockSpec(memory_space=pltpu.SMEM), vm, vm, vm, vm, vm],
         out_specs=(hb, hb),
         scratch_shapes=[pltpu.VMEM((LT // 2, LT, 2, NB, NB), jnp.float32), pltpu.VMEM((LT, STEPS, NB, NB), jnp.float32),
-                        pltpu.VMEM((LT * NB, STEPS * NB), jnp.bfloat16), pltpu.SemaphoreType.DMA((LT // 2,)),
+                        pltpu.VMEM((LT * NB, STEPS * NB), jnp.bfloat16),
                         pltpu.SemaphoreType.DMA((STEPS,)), pltpu.SemaphoreType.DMA((LT // 2,))],
-        compiler_params=pltpu.CompilerParams(vmem_limit_bytes=44 * 2**20),
+        compiler_params=pltpu.CompilerParams(vmem_limit_bytes=36 * 2**20),
         cost_estimate=pl.CostEstimate(flops=4_000_000_000, bytes_accessed=14 * 2**20, transcendentals=0),
         name="finish",
     )(place, a, rp, q, ub, linv)

time: 118 us -> 119 us (level)
  local copies, waits for them, and re-layouts: 5.09 us -> 8.25 us
  Pallas kernels: 32.6 us -> 30.6 us
    unnamed x2 -> x6, local copies, waits for them, and re-layouts: 0.01 us -> 3.16 us
    pallas_call x1, Pallas kernels: 8.27 us -> 6.85 us  [finish(): pl.pallas_call(finish_kernel, out_shape=(jax.ShapeDtypeStruct((LT, STEPS,...]
  transfers between devices with their start and end apart: 4 -> 4, of which waited for: 3 -> 3; matrix products, arithmetic and copies ran while one was open for 3% -> 3% of each run, Pallas kernels for 21% -> 20%
where the time goes in v8:
time: 119 us
  blocking collectives  32.9 us (28%)
  Pallas kernels  30.6 us (26%)
  starting transfers between devices  16.3 us (14%)
  between operations  14.9 us (13%)
  waiting for transfers between devices  13.3 us (11%)
  local copies, waits for them, and re-layouts  8.25 us (7%)
  other arithmetic  2.5 us (2%)
    pallas_call x1, Pallas kernels, chain(): pl.pallas_call(chain_kernel, out_shape=(jax.ShapeDtypeStruct((STEPS * NB,...  23.7 us
    all_to_all x1, blocking collectives, shards(): lax.all_to_all(first, 'col', 0, 0, tiled=True).reshape(16, LT, 8, NB)  17.9 us
    all_to_all x1, blocking collectives, shards(): mine = lax.all_to_all(lead, 'col', 0, 0, tiled=True)  15.1 us
    all_to_all x1, waiting for transfers between devices, shards(): lax.all_to_all(sent, 'row', 0, 0, tiled=True, axis_index_groups=groups)  10.4 us
    all_to_all x1, starting transfers between devices, shards(): lax.all_to_all(sent, 'row', 0, 0, tiled=True, axis_index_groups=groups)  8.19 us
    pallas_call x1, Pallas kernels, finish(): pl.pallas_call(finish_kernel, out_shape=(jax.ShapeDtypeStruct((LT, STEPS,...  6.85 us
    all_to_all x1, starting transfers between devices, shards(): down = lax.all_to_all(half, 'col', 0, 0, tiled=True)  4.43 us
    ppermute x1, starting transfers between devices, shards(): other = lax.ppermute(mine, 'row', [(i, i ^ 1) for i in range(16)])  3.62 us
  transfers between devices with their start and end apart: 4, of which 3 were waited for; matrix products, arithmetic and copies ran while one was open for 3% of the time, Pallas kernels for 20%

profile of v8, /device:TPU:1, one launch (start us, length us, event | category | flops | bytes accessed | tf_op | source)
XLA Modules:
  0.0 118.8 jit_solution(9003796708040216949)
XLA Ops:
  7.2 0.0 all-gather.3.cloned.1.call-start
  7.2 1.9 %slice.23 = f32[1,1,8,1,128,128]{5,4,3,2,1,0:T(8,128)} slice(f32[8,1,8,1,128,128]{5,4,3,2,1,0:T(8,128)} %param.1), slice={[0:1], [0:1], [0:8], [0:1], [0:128], [0:128]} | slice | bytes 1048576 | tf_op jit(solution)/shard_map/slice | solution.py:245
  9.1 0.0 all-gather.3.cloned.1.call-update
  9.1 1.1 copy_bitcast_fusion
  10.2 17.9 %all_to_all.24 = f32[16,64,128]{2,1,0:T(8,128)S(1)} all-to-all(f32[16,64,128]{2,1,0:T(8,128)S(1)} %copy_bitcast_fusion), channel_id=1, replica_groups=mesh['row'=16,'col'=16] {'col'}, dimensions={0} | all-to-all | bytes 1048576 | tf_op jit(solution)/shard_map/all_to_all | solution.py:247
  28.1 0.7 broadcast_in_dim.21
  28.8 8.2 %all-to-all-start.1 = ((f32[8,6,8,128]{3,2,1,0:T(8,128)}), f32[8,6,8,128]{3,2,1,0:T(8,128)S(1)}, u32[]{:S(2)}, u32[]{:S(2)}) async-start(f32[8,6,8,128]{3,2,1,0:T(8,128)} %broadcast_in_dim.21), calls=%async_computation.1 | async-start | bytes 393216 | tf_op jit(solution)/shard_map/all_to_all | solution.py:251
  37.0 0.6 abs_reduce_fusion
  38.4 10.4 %all-to-all-done.1.x_ref = f32[8,6,8,128]{3,2,1,0:T(8,128)S(1)} async-done(((f32[8,6,8,128]{3,2,1,0:T(8,128)}), f32[8,6,8,128]{3,2,1,0:T(8,128)S(1)}, u32[]{:S(2)}, u32[]{:S(2)}) %all-to-all-start.1) | async-done | bytes 196640 | tf_op jit(solution)/shard_map/all_to_all | solution.py:251
  48.9 0.1 spread.1
  48.9 1.4 %broadcast_in_dim.22 = f16[16,400,128]{2,1,0:T(8,128)(2,1)} broadcast(f16[400,128]{1,0:T(8,128)(2,1)S(1)} %concatenate.3), dimensions={1,2} | broadcast | bytes 1740800 | tf_op jit(solution)/shard_map/broadcast_in_dim | solution.py:253
  50.3 15.1 %all_to_all.25.mine_ref = f32[16,12,8,128]{3,2,1,0:T(8,128)S(1)} all-to-all(f32[16,12,8,128]{3,2,1,0:T(8,128)S(1)} %spread.1), channel_id=1, replica_groups=mesh['row'=16,'col'=16] {'col'}, dimensions={0} | all-to-all | bytes 1572864 | tf_op jit(solution)/shard_map/all_to_all | solution.py:254
  65.4 3.6 %collective-permute-start = (f32[16,12,8,128]{3,2,1,0:T(8,128)S(1)}, f32[16,12,8,128]{3,2,1,0:T(8,128)S(1)}, u32[]{:S(2)}, u32[]{:S(2)}) collective-permute-start(f32[16,12,8,128]{3,2,1,0:T(8,128)S(1)} %all_to_all.25.mine_ref), channel_id=1, source_target_pairs={{0,16},{16,0},{32,48},{48,32},{64,80},{80,64},{96,112},{112,96},{1... | collective-permute-start | bytes 2359304 | tf_op jit(solution)/shard_map/ppermute | solution.py:256
  69.0 0.1 pad_add_fusion.place_ref
  69.1 4.4 %all-to-all-start.3 = ((f16[16,400,128]{2,1,0:T(8,128)(2,1)}), f16[16,400,128]{2,1,0:T(8,128)(2,1)}, u32[]{:S(2)}, u32[]{:S(2)}) async-start(f16[16,400,128]{2,1,0:T(8,128)(2,1)} %broadcast_in_dim.22), calls=%async_computation.3 | async-start | bytes 3276800 | tf_op jit(solution)/shard_map/all_to_all | solution.py:257
  73.5 1.3 %all-gather.3.cloned.1.call-done = f32[16,1,8,1,128,128]{5,4,3,2,1,0:T(8,128)} async-done(((f32[1,1,8,1,128,128]{5,4,3,2,1,0:T(8,128)}), f32[16,1,8,1,128,128]{5,4,3,2,1,0:T(8,128)}) %all-gather.3.cloned.1.call-update) | async-done | bytes 8388624 | tf_op jit(solution)/shard_map/all_gather | solution.py:245
  74.8 23.7 %chain.1 = (bf16[768,768]{1,0:T(8,128)(2,1)S(1)}, f32[6,128,128]{2,1,0:T(8,128)S(1)}, bf16[768,1024]{1,0:T(8,128)(2,1)S(1)}, f32[1,1]{1,0:T(1,128)}) custom-call(s32[2]{0:T(128)S(1)} %pad_add_fusion.place_ref, f32[16,12,8,128]{3,2,1,0:T(8,128)S(1)} %all_to_all.25.mine_ref, f32[16,12,8,128]{3,2,1,0:T(8,128)S(1)} %collective-permute-done.other_ref, ...), custom_call_target="tpu_custom_call" | custom-call | flops 30000001024 | bytes 4194304 | tf_op jit(solution)/shard_map/chain/pallas_call | solution.py:127
  98.5 0.0 copy-start.1
  98.5 1.0 copy-done.1
  99.5 1.6 %all-to-all-done.3 = f16[16,400,128]{2,1,0:T(8,128)(2,1)} async-done(((f16[16,400,128]{2,1,0:T(8,128)(2,1)}), f16[16,400,128]{2,1,0:T(8,128)(2,1)}, u32[]{:S(2)}, u32[]{:S(2)}) %all-to-all-start.3) | async-done | bytes 1638432 | tf_op jit(solution)/shard_map/all_to_all | solution.py:257
  101.1 1.8 %convert_element_type.15.rp_ref = f32[16,400,128]{2,1,0:T(8,128)S(1)} convert(f16[16,400,128]{2,1,0:T(8,128)(2,1)} %all-to-all-done.3) | non-fusion elementwise | flops 819200 | bytes 4915200 | tf_op jit(solution)/shard_map/convert_element_type | solution.py:260
  102.9 0.9 copy-done
  103.8 1.3 %copy-done.2 = bf16[768,768]{1,0:T(8,128)(2,1)S(1)} copy-done((bf16[768,768]{1,0:T(8,128)(2,1)S(1)}, bf16[768,768]{1,0:T(8,128)(2,1)}, u32[]{:S(2)}) %copy-start.2) | copy-done | bytes 1179672
  105.1 6.9 %finish.1 = (f32[8,6,128,128]{3,2,1,0:T(8,128)}, f32[8,8,128,128]{3,2,1,0:T(8,128)}) custom-call(s32[2]{0:T(128)S(1)} %pad_add_fusion.place_ref, f32[8,8,128,128]{3,2,1,0:T(8,128)S(1)} %bitcast.24, f32[16,400,128]{2,1,0:T(8,128)S(1)} %convert_element_type.15.rp_ref, bf16[768,1024]{1,0:T(8,128)(2,1)S(1)} %get-tuple-element.25.q_ref, ...), custom_call_target="tpu_custom_call" | custom-call | flops 4000000000 | bytes 14680064 | tf_op jit(solution)/shard_map/finish/pallas_call | solution.py:201
  (7 shorter events, 0.1 us)
Async XLA Ops:
  7.2 67.6 %all-gather.3.cloned.1.call-start = ((), (), s32[]{:S(2)}) async-start(), calls=%async_computation.4 | async-start | bytes 8912896 | tf_op jit(solution)/shard_map/all_gather | solution.py:245
  28.8 20.0 %all-to-all-start.1 = ((f32[8,6,8,128]{3,2,1,0:T(8,128)}), f32[8,6,8,128]{3,2,1,0:T(8,128)S(1)}, u32[]{:S(2)}, u32[]{:S(2)}) async-start(f32[8,6,8,128]{3,2,1,0:T(8,128)} %broadcast_in_dim.21), calls=%async_computation.1 | async-start | bytes 393216 | tf_op jit(solution)/shard_map/all_to_all | solution.py:251
  65.4 8.1 %collective-permute-start = (f32[16,12,8,128]{3,2,1,0:T(8,128)S(1)}, f32[16,12,8,128]{3,2,1,0:T(8,128)S(1)}, u32[]{:S(2)}, u32[]{:S(2)}) collective-permute-start(f32[16,12,8,128]{3,2,1,0:T(8,128)S(1)} %all_to_all.25.mine_ref), channel_id=1, source_target_pairs={{0,16},{16,0},{32,48},{48,32},{64,80},{80,64},{96,112},{112,96},{1... | collective-permute-start | bytes 2359304 | tf_op jit(solution)/shard_map/ppermute | solution.py:256
  69.1 32.1 %all-to-all-start.3 = ((f16[16,400,128]{2,1,0:T(8,128)(2,1)}), f16[16,400,128]{2,1,0:T(8,128)(2,1)}, u32[]{:S(2)}, u32[]{:S(2)}) async-start(f16[16,400,128]{2,1,0:T(8,128)(2,1)} %broadcast_in_dim.22), calls=%async_computation.3 | async-start | bytes 3276800 | tf_op jit(solution)/shard_map/all_to_all | solution.py:257
  98.5 1.0 copy-start.1
  101.1 2.7 %copy-start = (f32[8,1,8,1,128,128]{5,4,3,2,1,0:T(8,128)S(1)}, f32[8,1,8,1,128,128]{5,4,3,2,1,0:T(8,128)}, u32[]{:S(2)}) copy-start(f32[8,1,8,1,128,128]{5,4,3,2,1,0:T(8,128)} %param.1) | copy-start | bytes 12582916
  103.8 1.3 %copy-start.2 = (bf16[768,768]{1,0:T(8,128)(2,1)S(1)}, bf16[768,768]{1,0:T(8,128)(2,1)}, u32[]{:S(2)}) copy-start(bf16[768,768]{1,0:T(8,128)(2,1)} %copy-done.1) | copy-start | bytes 3538948
Sparse Core Ops, SparseCore 0:
  10.4 64.3 all-gather.2
